TPU v7x, 256 devices: a whole 4x4x8 slice. The times are simulated.
256 devices in a mesh: seq: 32 (over x, y, core), vid: 8 (over z).
Axes of the slice: x: 4, y: 4, z: 8, core: 2. Of those that a mesh axis runs over, the one named last changes fastest.
Arguments:
- tokens: bfloat16 [262144, 768], P(('vid', 'seq')), parts along dimension 0, may hold values from -100 to 100
- latents: bfloat16 [4096, 768], P(('vid', 'seq')), parts along dimension 0, may hold values from -6 to 6
- read_weights: bfloat16 [4, 768, 768], P(None, 'seq'), may hold values from -1 to 1
- later_weights: bfloat16 [8, 768, 768], P(None, 'seq'), may hold values from -1 to 1
- head_scale: float32 [3, 12], replicated, may hold values from 1 to 40
Outputs:
- tokens_out: bfloat16 [262144, 768], P(('vid', 'seq')), parts along dimension 0
- latents_out: float32 [4096, 768], P(('vid', 'seq')), parts along dimension 0
There are 8 independent parts, one for each index of `vid`. A program takes and returns all parts, laid end to end along the dimension named above; an argument that names none is the same for every part. Nothing has to cross between parts.
All inputs are finite; a program needn't handle non-finite values.
Results may differ from a plain program's by a relative error of at most 0.01.
The roundings to bfloat16 on the way count: a program that leaves them out, or rounds other values in their place, can miss the bound.
Values may be sent and summed in bfloat16 or wider, within the bound.
No kernel may reach another device: no remote copies, remote signals or barrier semaphores. Data moves between devices by JAX's collectives and lax.ppermute only.
A program may use at most 64 MiB of HBM per device.

v0:
```python
import math

import jax
import jax.numpy as jnp
from jax import lax
from jax.sharding import PartitionSpec as P

HEADS = 12


epsilon = 1e-06


def norm_rows(values):
    values = values.astype(jnp.float32)
    return values * lax.rsqrt(jnp.mean(values * values, axis=-1, keepdims=True) + epsilon)


def head_norm(values, n_heads):
    by_head = values.reshape(values.shape[0], n_heads, values.shape[1] // n_heads)
    by_head = by_head * lax.rsqrt(jnp.mean(by_head * by_head, axis=-1, keepdims=True) + epsilon)
    return by_head.reshape(values.shape).astype(jnp.bfloat16)


def project(inputs, weight):
    return jnp.dot(inputs, weight, preferred_element_type=jnp.float32)


def head_cols(values, head_index, head_dim):
    return lax.dynamic_slice_in_dim(values, head_index * head_dim, head_dim, 1)


def inner(left, right):
    return lax.dot_general(
        left, right, (((1,), (1,)), ((), ())), preferred_element_type=jnp.float32
    )


def attend(queries, key_rows, val_rows, factors, n_heads):
    head_dim = queries.shape[1] // n_heads

    def attend_one_head(packed):
        head_index, factor = packed
        scores = inner(
            head_cols(queries, head_index, head_dim), head_cols(key_rows, head_index, head_dim)
        ) * (factor / math.sqrt(head_dim))
        row_top = jnp.max(scores, axis=1, keepdims=True)
        exp_scores = jnp.exp(scores - row_top)
        weights = (exp_scores / jnp.sum(exp_scores, axis=1, keepdims=True)).astype(jnp.bfloat16)
        return jnp.dot(
            weights, head_cols(val_rows, head_index, head_dim), preferred_element_type=jnp.float32
        )

    results = lax.map(attend_one_head, (jnp.arange(n_heads, dtype=jnp.int32), factors))
    return results.transpose(1, 0, 2).reshape(queries.shape).astype(jnp.bfloat16)


def read_parts(queries, key_rows, val_rows, factors, n_heads):
    head_dim = queries.shape[1] // n_heads

    def read_one_head(packed):
        head_index, factor = packed
        scores = inner(
            head_cols(queries, head_index, head_dim), head_cols(key_rows, head_index, head_dim)
        ) * (factor / math.sqrt(head_dim))
        row_top = jnp.max(scores, axis=1)
        exp_scores = jnp.exp(scores - row_top[:, None])
        totals = jnp.sum(exp_scores, axis=1)
        summed = jnp.dot(
            exp_scores.astype(jnp.bfloat16),
            head_cols(val_rows, head_index, head_dim),
            preferred_element_type=jnp.float32,
        )
        return (summed.astype(jnp.bfloat16), row_top, totals)

    return lax.map(read_one_head, (jnp.arange(n_heads, dtype=jnp.int32), factors))


def shards(tokens, latents, read_weights, later_weights, head_scale):
    own_rows = latents.shape[0]
    width = tokens.shape[1]
    read_full, later_full, lat_stack = (
        lax.all_gather(read_weights, "seq", axis=1, tiled=True),
        lax.all_gather(later_weights, "seq", axis=1, tiled=True),
        lax.all_gather(latents[None], "seq", axis=1, tiled=True),
    )
    tok_normed = norm_rows(tokens).astype(jnp.bfloat16)
    read_q = head_norm(project(norm_rows(lat_stack[0]).astype(jnp.bfloat16), read_full[0]), HEADS)
    read_k = head_norm(project(tok_normed, read_full[1]), HEADS)
    read_v = project(tok_normed, read_full[2]).astype(jnp.bfloat16)
    partials, row_tops, totals = read_parts(read_q, read_k, read_v, head_scale[0], HEADS)
    row_best = lax.pmax(row_tops, "seq")
    rescale = jnp.exp(row_tops - row_best)
    summed, weight_sum = (
        lax.psum_scatter(
            (partials.astype(jnp.float32) * rescale[..., None]).astype(jnp.bfloat16),
            "seq",
            scatter_dimension=1,
            tiled=True,
        ).astype(jnp.float32),
        lax.psum_scatter(
            (totals * rescale).astype(jnp.bfloat16), "seq", scatter_dimension=1, tiled=True
        ).astype(jnp.float32),
    )
    read_mixed = summed / weight_sum[..., None]
    read_mix = read_mixed.transpose(1, 0, 2).reshape(own_rows, width).astype(jnp.bfloat16)
    lat_one = latents.astype(jnp.float32) + project(read_mix, read_full[3])
    self_normed = norm_rows(lat_one).astype(jnp.bfloat16)
    self_q = head_norm(project(self_normed, later_full[0]), HEADS)
    self_k = head_norm(project(self_normed, later_full[1]), HEADS)
    self_v = project(self_normed, later_full[2]).astype(jnp.bfloat16)
    all_k, all_v = (
        lax.all_gather(self_k, "seq", axis=0, tiled=True),
        lax.all_gather(self_v, "seq", axis=0, tiled=True),
    )
    latents_out = lat_one + project(
        attend(self_q, all_k, all_v, head_scale[1], HEADS), later_full[3]
    )
    write_in = lax.all_gather(
        norm_rows(latents_out).astype(jnp.bfloat16), "seq", axis=0, tiled=True
    )
    write_q = head_norm(project(tok_normed, later_full[4]), HEADS)
    write_k = head_norm(project(write_in, later_full[5]), HEADS)
    write_v = project(write_in, later_full[6]).astype(jnp.bfloat16)
    tokens_out = (
        tokens.astype(jnp.float32)
        + project(attend(write_q, write_k, write_v, head_scale[2], HEADS), later_full[7])
    ).astype(jnp.bfloat16)
    return (tokens_out, latents_out)


def solution(mesh):
    placed = (
        P(("vid", "seq"), None),
        P(("vid", "seq"), None),
        P(None, "seq", None),
        P(None, "seq", None),
        P(),
    )
    return jax.shard_map(
        shards,
        mesh=mesh,
        in_specs=placed,
        out_specs=(P(("vid", "seq"), None), P(("vid", "seq"), None)),
        check_vma=False,
    )
```

profile of v0, /device:TPU:1, one launch (start us, length us, event | category | flops | bytes accessed | tf_op | source)
XLA Modules:
  0.0 756.3 jit_solution(18415992514651537995)
XLA Ops:
  8.0 26.7 %all-gather = bf16[512,768]{1,0:T(8,128)(2,1)S(1)} all-gather(bf16[16,768]{1,0:T(8,128)(2,1)} %param.12), channel_id=2, replica_groups=mesh['seq'=32,'vid'=8] {'seq'}, dimensions={0}, use_global_device_ids=true | all-gather | bytes 811008 | tf_op jit(solution)/shard_map/all_gather | solution.py:85
  35.3 31.5 %all-gather.6.cloned.1.call-done = bf16[4,768,768]{2,1,0:T(8,128)(2,1)} async-done(((bf16[4,24,768]{2,1,0:T(8,128)(2,1)}), bf16[4,768,768]{2,1,0:T(8,128)(2,1)}) %all-gather.6.cloned.1.call-update) | async-done | bytes 4718608 | tf_op jit(solution)/shard_map/all_gather | solution.py:83
  66.9 1.8 slice_bitcast_fusion.15
  68.6 1.5 copy.64
  70.1 4.9 multiply_reduce_fusion.2
  77.6 1.6 multiply_convert_fusion
  80.6 3.9 convolution_convert_fusion.1
  84.5 80.6 %while.34 = (s32[]{:T(128)}, bf16[12,512,64]{1,2,0:T(8,128)(2,1)}, f32[12,512]{1,0:T(8,128)S(1)}, f32[12,512]{1,0:T(8,128)S(1)}, s32[12]{0:T(128)S(1)}, /*index=...) while((s32[]{:T(128)}, bf16[12,512,64]{1,2,0:T(8,128)(2,1)}, ...), condition=%wide.region_8.9_spmd, body=%wide.region_5.8_spmd.sunk | while | flops 138443776 | bytes 6834919 | solution.py:76
  87.0 1.4 multiply_reduce_fusion.12
  89.0 2.2 fusion.87
  93.7 1.4 multiply_reduce_fusion.12
  95.7 2.2 fusion.87
  100.4 1.4 multiply_reduce_fusion.12
  102.4 2.2 fusion.87
  107.1 1.4 multiply_reduce_fusion.12
  109.1 2.2 fusion.87
  113.8 1.5 multiply_reduce_fusion.12
  115.9 2.2 fusion.87
  120.6 1.4 multiply_reduce_fusion.12
  122.6 2.2 fusion.87
  127.3 1.4 multiply_reduce_fusion.12
  129.3 2.2 fusion.87
  134.0 1.5 multiply_reduce_fusion.12
  136.0 2.2 fusion.87
  140.7 1.5 multiply_reduce_fusion.12
  142.7 2.2 fusion.87
  147.4 1.5 multiply_reduce_fusion.12
  149.5 2.2 fusion.87
  154.2 1.4 multiply_reduce_fusion.12
  156.2 2.2 fusion.87
  160.9 1.5 multiply_reduce_fusion.12
  162.9 2.2 fusion.87
  165.1 120.9 %pmax.7 = f32[12,512]{1,0:T(8,128)S(1)} all-reduce(f32[12,512]{1,0:T(8,128)S(1)} %get-tuple-element.126), channel_id=1, replica_groups=mesh['seq'=32,'vid'=8] {'seq'}, use_global_device_ids=true, to_apply=%region_9.10 | all-reduce | flops 6144 | bytes 49152 | tf_op jit(solution)/shard_map/pmax | solution.py:92
  286.9 1.3 multiply_convert_fusion.3
  288.2 2.9 copy.67
  291.7 75.5 %reduce-scatter.7.cloned.1.call-done = bf16[16,12]{1,0:T(8,128)(2,1)} async-done(((bf16[512,12]{1,0:T(8,128)(2,1)}), bf16[16,12]{1,0:T(8,128)(2,1)}) %reduce-scatter.7.cloned.1.call-update) | async-done | bytes 400
  368.1 89.2 %reduce-scatter.5.cloned.1.call-done = bf16[12,16,64]{2,0,1:T(8,128)(2,1)} async-done(((bf16[12,512,64]{2,0,1:T(8,128)(2,1)}), bf16[12,16,64]{2,0,1:T(8,128)(2,1)}) %reduce-scatter.5.cloned.1.call-update) | async-done | bytes 24592 | tf_op jit(solution)/shard_map/reduce_scatter | solution.py:95
  458.3 1.7 multiply_reduce_fusion.9
  461.3 60.3 %all-gather.4.cloned.1.call-done = bf16[8,768,768]{2,1,0:T(8,128)(2,1)} async-done(((bf16[8,24,768]{2,1,0:T(8,128)(2,1)}), bf16[8,768,768]{2,1,0:T(8,128)(2,1)}) %all-gather.4.cloned.1.call-update) | async-done | bytes 9437200 | tf_op jit(solution)/shard_map/all_gather | solution.py:84
  521.6 3.7 slice_bitcast_fusion.9
  525.2 2.4 copy.71
  527.6 1.9 multiply_reduce_fusion.6
  530.3 1.5 convert_element_type.154
  531.8 27.0 %all_gather.21 = bf16[512,768]{1,0:T(8,128)(2,1)} all-gather(bf16[16,768]{1,0:T(8,128)(2,1)} %convert_element_type.154), channel_id=1, replica_groups=mesh['seq'=32,'vid'=8] {'seq'}, dimensions={0}, use_global_device_ids=true | all-gather | bytes 811008 | tf_op jit(solution)/shard_map/all_gather | solution.py:113
  558.8 1.6 fusion.46
  560.3 25.4 %all_gather.22 = bf16[512,768]{1,0:T(8,128)(2,1)} all-gather(bf16[16,768]{1,0:T(8,128)(2,1)S(1)} %fusion.46), channel_id=1, replica_groups=mesh['seq'=32,'vid'=8] {'seq'}, dimensions={0}, use_global_device_ids=true | all-gather | bytes 811008 | tf_op jit(solution)/shard_map/all_gather | solution.py:114
  585.7 1.4 copy.69
  587.2 1.9 multiply_reduce_fusion.7
  589.4 60.8 %while.35 = (s32[]{:T(128)}, bf16[12,16,64]{2,1,0:T(8,128)(2,1)S(1)}, s32[12]{0:T(128)S(1)}, bf16[16,768]{1,0:T(8,128)(2,1)S(1)}, bf16[512,768]{1,0:T(8,128)(2,1...) while((s32[]{:T(128)}, ...), condition=%wide.region_18.19_spmd, body=%wide.region_15.18_spmd.sunk | while | flops 2154471 | bytes 376203 | solution.py:54
  650.4 1.7 multiply_reduce_fusion.8
  652.1 25.9 %all_gather.23 = bf16[512,768]{1,0:T(8,128)(2,1)} all-gather(bf16[16,768]{1,0:T(8,128)(2,1)S(1)} %multiply_convert_fusion.7), channel_id=1, replica_groups=mesh['seq'=32,'vid'=8] {'seq'}, dimensions={0}, use_global_device_ids=true | all-gather | bytes 811008 | tf_op jit(solution)/shard_map/all_gather | solution.py:119
  678.7 3.1 multiply_reduce_fusion.4
  681.8 1.4 copy.62
  683.3 2.9 multiply_reduce_fusion.3
  687.6 2.0 convolution_convert_fusion.2
  689.7 55.2 %while.36 = (s32[]{:T(128)}, bf16[12,1024,64]{1,2,0:T(8,128)(2,1)}, s32[12]{0:T(128)S(1)}, bf16[1024,768]{0,1:T(8,128)(2,1)S(1)}, bf16[512,768]{0,1:T(8,128)(2,1...) while((s32[]{:T(128)}, bf16[12,1024,64]{1,2,0:T(8,128)(2,1)}, ...), condition=%wide.region_24.25_spmd, body=%wide.region_21.24_spmd.sunk | while | flops 138934272 | bytes 6904019 | solution.py:54
  697.6 1.3 fusion.95
  706.8 1.3 fusion.95
  716.0 1.3 fusion.95
  720.6 1.3 fusion.95
  725.2 1.2 fusion.95
  729.8 1.3 fusion.95
  743.6 1.3 fusion.95
  744.9 4.8 fusion.34
  (247 shorter events, 110.9 us)
Async XLA Ops:
  7.2 27.7 %copy-start.1 = (bf16[1024,768]{1,0:T(8,128)(2,1)S(1)}, bf16[1024,768]{1,0:T(8,128)(2,1)}, u32[]{:S(2)}) copy-start(bf16[1024,768]{1,0:T(8,128)(2,1)} %param.11) | copy-start | bytes 4718596
  7.2 59.7 %all-gather.6.cloned.1.call-start = ((), (), s32[]{:S(2)}) async-start(), calls=%async_computation.3 | async-start | bytes 4866048 | tf_op jit(solution)/shard_map/all_gather | solution.py:83
  7.9 359.3 %reduce-scatter.7.cloned.1.call-start = ((), (), s32[]{:S(2)}) async-start(), calls=%async_computation.5 | async-start | bytes 135168
  8.0 27.3 %copy-start.11 = (f32[3,12]{1,0:T(4,128)S(1)}, f32[3,12]{1,0:T(4,128)}, u32[]{:S(2)}) copy-start(f32[3,12]{1,0:T(4,128)} %param.15) | copy-start | bytes 436
  75.7 1.9 copy-start
  79.2 1.4 copy-start.2
  286.9 170.4 %reduce-scatter.5.cloned.1.call-start = ((), (), s32[]{:S(2)}) async-start(), calls=%async_computation.4 | async-start | bytes 2162688 | tf_op jit(solution)/shard_map/reduce_scatter | solution.py:95
  291.1 167.2 %copy-start.9 = (bf16[16,768]{1,0:T(8,128)(2,1)S(1)}, bf16[16,768]{1,0:T(8,128)(2,1)}, u32[]{:S(2)}) copy-start(bf16[16,768]{1,0:T(8,128)(2,1)} %param.12) | copy-start | bytes 73732
  291.1 230.5 %all-gather.4.cloned.1.call-start = ((), (), s32[]{:S(2)}) async-start(), calls=%async_computation.2 | async-start | bytes 9732096 | tf_op jit(solution)/shard_map/all_gather | solution.py:84
  460.0 0.6 copy-start.6
  587.2 2.2 copy-start.10
  589.1 61.3 %copy-start.7 = (f32[16,768]{1,0:T(8,128)S(1)}, f32[16,768]{1,0:T(8,128)}, u32[]{:S(2)}) copy-start(f32[16,768]{1,0:T(8,128)} %copy-done.6) | copy-start | bytes 147460
  652.0 26.0 %copy-start.8 = (f32[16,768]{1,0:T(8,128)}, f32[16,768]{1,0:T(8,128)S(1)}, u32[]{:S(2)}) copy-start(f32[16,768]{1,0:T(8,128)S(1)} %get-tuple-element.286) | copy-start | bytes 147460
  681.7 1.5 copy-start.3
  683.3 3.0 copy-start.4
  686.5 1.1 copy-start.5
Sparse Core Ops, SparseCore 0:
  10.7 56.1 all-gather.5
  287.0 80.1 reduce-scatter.6
  371.1 86.1 reduce-scatter.4
  459.8 61.7 all-gather.3
where the time goes:
time: 759 us; the launch traced here: 756 us
  waiting for transfers between devices  258 us (34%)
  blocking collectives  226 us (30%)
  matrix products  124 us (16%)
  local copies, waits for them, and re-layouts  68 us (9%)
  loops' own time  46.7 us (6%)
  other arithmetic  19.4 us (3%)
  between operations  14.1 us (2%)
    pmax x1, blocking collectives, shards(): row_best = lax.pmax(row_tops, 'seq')  121 us
    reduce_scatter x1, waiting for transfers between devices, shards(): lax.psum_scatter((partials.astype(jnp.float32) * rescale[..., None]).asty...  89.2 us
    unnamed x5, waiting for transfers between devices  76.8 us
    all_gather x1, waiting for transfers between devices, shards(): lax.all_gather(later_weights, 'seq', axis=1, tiled=True)  60.3 us
    dynamic_slice x72, local copies, waits for them, and re-layouts, read_parts(): lax.map(read_one_head, (jnp.arange(n_heads, dtype=jnp.int32), factors))  43 us
    dot_general x36, matrix products, inner(): lax.dot_general(left, right, (((1,), (1,)), ((), ())), preferred_element_...  38.2 us
    another operation x2, loops' own time, attend(): lax.map(attend_one_head, (jnp.arange(n_heads, dtype=jnp.int32), factors))  31.6 us
    all_gather x1, waiting for transfers between devices, shards(): lax.all_gather(read_weights, 'seq', axis=1, tiled=True)  31.5 us
  transfers between devices with their start and end apart: 4, of which 4 were waited for; matrix products, arithmetic and copies ran while one was open for 1% of the time, Pallas kernels for 0%

commit v1 on v0

v1 whole, which is shorter than its diff:
```python
import functools
import math

import jax
import jax.numpy as jnp
from jax import lax
from jax.experimental import pallas as pl
from jax.experimental.pallas import tpu as pltpu
from jax.sharding import PartitionSpec as P

HEADS = 12
HEAD_DIM = 64
PAIR = 2 * HEAD_DIM
EPSILON = 1e-06
LOG2E = math.log2(math.e)
BF16 = jnp.bfloat16
F32 = jnp.float32
VMEM_LIMIT = 56 * 1024 * 1024
PIECE = 20
ODD_TOTALS = 12
EVEN_TOTALS = 64


def norm_rows(values):
    values = values.astype(F32)
    return values * lax.rsqrt(jnp.mean(values * values, axis=-1, keepdims=True) + EPSILON)


def dot(left, right):
    return jnp.dot(left, right, preferred_element_type=F32)


def dot_nt(left, right):
    return lax.dot_general(left, right, (((1,), (1,)), ((), ())), preferred_element_type=F32)


def head_mean_matrix():
    rows = lax.broadcasted_iota(jnp.int32, (256, 256), 0) // HEAD_DIM
    cols = lax.broadcasted_iota(jnp.int32, (256, 256), 1) // HEAD_DIM
    return jnp.where(rows == cols, 1.0 / HEAD_DIM, 0.0).astype(BF16)


def head_norm(values, mean_matrix):
    squares = values * values
    high = squares.astype(BF16)
    low = (squares - high.astype(F32)).astype(BF16)
    parts = []
    for start in range(0, values.shape[1], 256):
        cols = slice(start, start + 256)
        mean = dot(high[:, cols], mean_matrix) + dot(low[:, cols], mean_matrix)
        parts.append((values[:, cols] * lax.rsqrt(mean + EPSILON)).astype(BF16))
    return jnp.concatenate(parts, axis=1)


def first_half(shape):
    return lax.broadcasted_iota(jnp.int32, shape, 1) % PAIR < HEAD_DIM


def row_blocks(n_rows, block, body):
    def step(i, carry):
        body(pl.ds(pl.multiple_of(i * block, block), block))
        return carry

    lax.fori_loop(0, n_rows // block, step, 0)


def project_heads(x_ref, weight, mean_matrix, out_ref, block=256):
    def body(rows):
        out_ref[rows, :] = head_norm(dot(x_ref[rows, :], weight[...]), mean_matrix)

    row_blocks(x_ref.shape[0], block, body)


def project_values(x_ref, weight, even_ref, odd_ref, block=256):
    def body(rows):
        values = dot(x_ref[rows, :], weight[...]).astype(BF16)
        mask = first_half(values.shape)
        one = jnp.ones_like(values)
        even_ref[rows, :] = jnp.where(mask, values, one)
        odd_ref[rows, :] = jnp.where(mask, one, values)

    row_blocks(x_ref.shape[0], block, body)


def pair_parts(queries, keys, even, odd, even_factor, odd_factor):
    mask = first_half(queries.shape)
    zero = jnp.zeros_like(queries)
    scores_even = dot_nt(jnp.where(mask, queries, zero), keys)
    scores_odd = dot_nt(jnp.where(mask, zero, queries), keys)
    top_even = jnp.max(scores_even, axis=1, keepdims=True)
    exp_even = jnp.exp2((scores_even - top_even) * (even_factor * LOG2E)).astype(BF16)
    top_odd = jnp.max(scores_odd, axis=1, keepdims=True)
    exp_odd = jnp.exp2((scores_odd - top_odd) * (odd_factor * LOG2E)).astype(BF16)
    return top_even, top_odd, dot(exp_even, even), dot(exp_odd, odd)


def factors(scale_ref, stage, pair):
    root = math.sqrt(HEAD_DIM)
    return scale_ref[stage, 2 * pair] / root, scale_ref[stage, 2 * pair + 1] / root


def attend(q_ref, k_ref, even_ref, odd_ref, scale_ref, stage, out_ref, block=256):
    n_blocks = q_ref.shape[0] // block

    def step(i, carry):
        pair, row = i // n_blocks, i % n_blocks
        cols = pl.ds(pl.multiple_of(pair * PAIR, PAIR), PAIR)
        rows = pl.ds(pl.multiple_of(row * block, block), block)
        _, _, even, odd = pair_parts(
            q_ref[rows, cols],
            k_ref[:, cols],
            even_ref[:, cols],
            odd_ref[:, cols],
            *factors(scale_ref, stage, pair),
        )
        mask = first_half(even.shape)
        summed = jnp.where(mask, even, odd)
        total = pltpu.roll(jnp.where(mask, odd, even), HEAD_DIM, 1)
        out_ref[rows, cols] = (summed / total).astype(BF16)
        return carry

    lax.fori_loop(0, n_blocks * (HEADS // 2), step, 0)


def read_kernel(
    tok_ref, lat_ref, weight_ref, scale_ref, out_ref, q_ref, k_ref, even_ref, odd_ref, extra_ref
):
    mean_matrix = head_mean_matrix()
    width = tok_ref.shape[1]
    project_heads(lat_ref, weight_ref.at[0], mean_matrix, q_ref)
    project_heads(tok_ref, weight_ref.at[1], mean_matrix, k_ref)
    project_values(tok_ref, weight_ref.at[2], even_ref, odd_ref)
    extra_ref[...] = jnp.zeros_like(extra_ref)
    block = 256
    n_blocks = lat_ref.shape[0] // block

    def step(i, carry):
        pair, row = i // n_blocks, i % n_blocks
        cols = pl.ds(pl.multiple_of(pair * PAIR, PAIR), PAIR)
        rows = pl.ds(pl.multiple_of(row * block, block), block)
        even_factor, odd_factor = factors(scale_ref, 0, pair)
        top_even, top_odd, even, odd = pair_parts(
            q_ref[rows, cols],
            k_ref[:, cols],
            even_ref[:, cols],
            odd_ref[:, cols],
            even_factor,
            odd_factor,
        )
        out_ref[rows, cols] = jnp.where(first_half(even.shape), even, odd).astype(BF16)
        lane = lax.broadcasted_iota(jnp.int32, even.shape, 1)
        extra = extra_ref[rows, :]
        extra = jnp.where(lane == 2 * pair, top_even * even_factor, extra)
        extra = jnp.where(lane == 2 * pair + 1, top_odd * odd_factor, extra)
        extra = jnp.where(lane == EVEN_TOTALS + pair, even, extra)
        extra = jnp.where(lane == ODD_TOTALS + pair, odd, extra)
        extra_ref[rows, :] = extra
        return carry

    lax.fori_loop(0, n_blocks * (HEADS // 2), step, 0)
    extra = extra_ref[...]
    high = extra.astype(BF16).astype(F32)
    mid = (extra - high).astype(BF16).astype(F32)
    low = extra - high - mid
    packed = high + pltpu.roll(mid, PIECE, 1) + pltpu.roll(low, 2 * PIECE, 1)
    out_ref[:, width:] = packed.astype(BF16)


def combine_kernel(part_ref, out_ref, *, slabs):
    width = out_ref.shape[-1]
    own_rows = out_ref.shape[1]
    lane = lax.broadcasted_iota(jnp.int32, (PAIR, width), 0)
    head = lax.broadcasted_iota(jnp.int32, (PAIR, width), 1) // HEAD_DIM
    total_lane = jnp.where(head % 2 == 0, EVEN_TOTALS, ODD_TOTALS) + head // 2
    pick_top = jnp.zeros((PAIR, width), F32)
    pick_total = jnp.zeros((PAIR, width), F32)
    for piece in range(3):
        pick_top = jnp.where(lane == head + piece * PIECE, 1.0, pick_top)
        pick_total = jnp.where(lane == total_lane + piece * PIECE, 1.0, pick_total)
    extra = part_ref[:, width:]
    shape = (slabs, own_rows, width)
    tops = dot(extra, pick_top.astype(BF16)).reshape(shape)
    totals = dot(extra, pick_total.astype(BF16)).reshape(shape)
    rescale = jnp.exp(tops - jnp.max(tops, axis=0, keepdims=True))
    sums = part_ref[:, :width].astype(F32).reshape(shape)
    mixed = jnp.sum(rescale * sums, axis=0) / jnp.sum(rescale * totals, axis=0)
    out_ref[...] = jnp.broadcast_to(mixed.astype(BF16)[None], out_ref.shape)


def write_kernel(
    index_ref,
    scale_ref,
    mix_ref,
    lat_ref,
    out_weight_ref,
    weight_ref,
    raw_ref,
    tok_ref,
    tok_out_ref,
    lat_out_ref,
    stream_ref,
    normed_ref,
    q_ref,
    k_ref,
    even_ref,
    odd_ref,
    att_ref,
    write_q_ref,
    write_att_ref,
):
    mean_matrix = head_mean_matrix()
    n_lat = lat_ref.shape[0]
    own_rows = lat_out_ref.shape[0]

    def first(rows):
        lat_one = lat_ref[rows, :].astype(F32) + dot(mix_ref[rows, :], out_weight_ref[...])
        stream_ref[rows, :] = lat_one
        normed_ref[rows, :] = norm_rows(lat_one).astype(BF16)

    row_blocks(n_lat, 256, first)
    project_heads(normed_ref, weight_ref.at[0], mean_matrix, q_ref)
    project_heads(normed_ref, weight_ref.at[1], mean_matrix, k_ref)
    project_values(normed_ref, weight_ref.at[2], even_ref, odd_ref)
    attend(q_ref, k_ref, even_ref, odd_ref, scale_ref, 1, att_ref)

    def second(rows):
        lat_two = stream_ref[rows, :] + dot(att_ref[rows, :], weight_ref[3])
        stream_ref[rows, :] = lat_two
        normed_ref[rows, :] = norm_rows(lat_two).astype(BF16)

    row_blocks(n_lat, 256, second)
    own = pl.ds(pl.multiple_of(index_ref[0] * own_rows, own_rows), own_rows)
    lat_out_ref[...] = stream_ref[own, :]
    project_heads(normed_ref, weight_ref.at[5], mean_matrix, k_ref)
    project_values(normed_ref, weight_ref.at[6], even_ref, odd_ref)
    project_heads(tok_ref, weight_ref.at[4], mean_matrix, write_q_ref)
    attend(write_q_ref, k_ref, even_ref, odd_ref, scale_ref, 2, write_att_ref)

    def last(rows):
        update = dot(write_att_ref[rows, :], weight_ref[7])
        tok_out_ref[rows, :] = (raw_ref[rows, :].astype(F32) + update).astype(BF16)

    row_blocks(raw_ref.shape[0], 256, last)


IN_VMEM = pl.BlockSpec(memory_space=pltpu.VMEM)
IN_SMEM = pl.BlockSpec(memory_space=pltpu.SMEM)


def shards(tokens, latents, read_weights, later_weights, head_scale):
    n_tok, width = tokens.shape
    own_rows = latents.shape[0]
    slabs = lax.axis_size("seq")
    n_lat = own_rows * slabs
    read_full = lax.all_gather(read_weights, "seq", axis=1, tiled=True)
    later_full = lax.all_gather(later_weights, "seq", axis=1, tiled=True)
    lat_full = lax.all_gather(latents, "seq", axis=0, tiled=True)
    tok_normed = norm_rows(tokens).astype(BF16)
    lat_normed = norm_rows(lat_full).astype(BF16)
    params = pltpu.CompilerParams(vmem_limit_bytes=VMEM_LIMIT)
    parts = pl.pallas_call(
        read_kernel,
        name="read",
        out_shape=jax.ShapeDtypeStruct((n_lat, width + PAIR), BF16),
        in_specs=[IN_VMEM, IN_VMEM, IN_VMEM, IN_SMEM],
        out_specs=IN_VMEM,
        scratch_shapes=[
            pltpu.VMEM((n_lat, width), BF16),
            pltpu.VMEM((n_tok, width), BF16),
            pltpu.VMEM((n_tok, width), BF16),
            pltpu.VMEM((n_tok, width), BF16),
            pltpu.VMEM((n_lat, PAIR), F32),
        ],
        compiler_params=params,
        cost_estimate=pl.CostEstimate(
            flops=20_000_000_000, bytes_accessed=8_000_000, transcendentals=6_300_000
        ),
    )(tok_normed, lat_normed, read_full[:3], head_scale)
    parts = lax.all_to_all(parts, "seq", 0, 0, tiled=True)
    mixed = pl.pallas_call(
        functools.partial(combine_kernel, slabs=slabs),
        name="combine",
        out_shape=jax.ShapeDtypeStruct((slabs, own_rows, width), BF16),
        in_specs=[IN_VMEM],
        out_specs=IN_VMEM,
        compiler_params=params,
    )(parts)
    mixed = lax.all_to_all(mixed, "seq", 0, 0, tiled=True).reshape(n_lat, width)
    index = lax.axis_index("seq").astype(jnp.int32).reshape(1)
    return pl.pallas_call(
        write_kernel,
        name="write",
        out_shape=(
            jax.ShapeDtypeStruct(tokens.shape, BF16),
            jax.ShapeDtypeStruct(latents.shape, F32),
        ),
        in_specs=[IN_SMEM, IN_SMEM] + [IN_VMEM] * 6,
        out_specs=(IN_VMEM, IN_VMEM),
        scratch_shapes=[
            pltpu.VMEM((n_lat, width), F32),
            pltpu.VMEM((n_lat, width), BF16),
            pltpu.VMEM((n_lat, width), BF16),
            pltpu.VMEM((n_lat, width), BF16),
            pltpu.VMEM((n_lat, width), BF16),
            pltpu.VMEM((n_lat, width), BF16),
            pltpu.VMEM((n_lat, width), BF16),
            pltpu.VMEM((n_tok, width), BF16),
            pltpu.VMEM((n_tok, width), BF16),
        ],
        compiler_params=params,
    )(index, head_scale, mixed, lat_full, read_full[3], later_full, tokens, tok_normed)


def solution(mesh):
    placed = (
        P(("vid", "seq"), None),
        P(("vid", "seq"), None),
        P(None, "seq", None),
        P(None, "seq", None),
        P(),
    )
    return jax.shard_map(
        shards,
        mesh=mesh,
        in_specs=placed,
        out_specs=(P(("vid", "seq"), None), P(("vid", "seq"), None)),
        check_vma=False,
    )
```

time: 759 us -> 190 us (0.25)
  waiting for transfers between devices: 258 us -> 45.2 us
  blocking collectives: 226 us -> 49 us
  matrix products: 124 us -> 0 us
  Pallas kernels: 0 us -> 65.6 us
  local copies, waits for them, and re-layouts: 68 us -> 7.22 us
  loops' own time: 46.7 us -> 0 us
  other arithmetic: 19.4 us -> 3.22 us
    dot_general x84 -> x0, matrix products: 124 us -> none  [the longest x36 38.2 us: inner(): lax.dot_general(left, right, (((1,), (1,)), ((), ())), preferred_element_...]
    pmax x1 -> x0, blocking collectives: 121 us -> none  [shards(): row_best = lax.pmax(row_tops, 'seq')]
    reduce_scatter x1 -> x0, waiting for transfers between devices: 89.2 us -> none  [shards(): lax.psum_scatter((partials.astype(jnp.float32) * rescale[..., None]).asty...]
    all_gather x4 -> x1, blocking collectives: 105 us -> 27.3 us  [shards(): lat_full = lax.all_gather(latents, 'seq', axis=0, tiled=True)]
    unnamed x5 -> x2, waiting for transfers between devices: 76.8 us -> 1.38 us
    pallas_call x0 -> x3, Pallas kernels: none -> 65.6 us  [the longest x1 42.5 us: shards(): pl.pallas_call(write_kernel, name='write', out_shape=(jax.ShapeDtypeStruc...]
    all_gather x2, waiting for transfers between devices: 91.8 us -> 28 us  [the longest x1 28 us: shards(): read_full = lax.all_gather(read_weights, 'seq', axis=1, tiled=True)]
    another operation x3 -> x0, loops' own time: 46.7 us -> none  [the longest x2 31.6 us: attend(): lax.map(attend_one_head, (jnp.arange(n_heads, dtype=jnp.int32), factors))]
  transfers between devices with their start and end apart: 4 -> 3, of which waited for: 4 -> 2; matrix products, arithmetic and copies ran while one was open for 1% -> 5% of each run, Pallas kernels for 0% -> 12%
where the time goes in v1:
time: 190 us
  Pallas kernels  65.6 us (35%)
  blocking collectives  49 us (26%)
  waiting for transfers between devices  45.2 us (24%)
  between operations  14.1 us (7%)
  local copies, waits for them, and re-layouts  7.22 us (4%)
  starting transfers between devices  5.25 us (3%)
  other arithmetic  3.22 us (2%)
    pallas_call x1, Pallas kernels, shards(): pl.pallas_call(write_kernel, name='write', out_shape=(jax.ShapeDtypeStruc...  42.5 us
    all_gather x1, waiting for transfers between devices, shards(): read_full = lax.all_gather(read_weights, 'seq', axis=1, tiled=True)  28 us
    all_gather x1, blocking collectives, shards(): lat_full = lax.all_gather(latents, 'seq', axis=0, tiled=True)  27.3 us
    all_to_all x1, blocking collectives, shards(): parts = lax.all_to_all(parts, 'seq', 0, 0, tiled=True)  21.7 us
    pallas_call x1, Pallas kernels, shards(): pl.pallas_call(read_kernel, name='read', out_shape=jax.ShapeDtypeStruct((...  20.2 us
    all_to_all x1, waiting for transfers between devices, shards(): mixed = lax.all_to_all(mixed, 'seq', 0, 0, tiled=True).reshape(n_lat, width)  15.9 us
    all_to_all x1, starting transfers between devices, shards(): mixed = lax.all_to_all(mixed, 'seq', 0, 0, tiled=True).reshape(n_lat, width)  5.18 us
    slice x1, local copies, waits for them, and re-layouts, shards(): read_full[:3]  3.96 us
  transfers between devices with their start and end apart: 3, of which 2 were waited for; matrix products, arithmetic and copies ran while one was open for 5% of the time, Pallas kernels for 12%

profile of v1, /device:TPU:1, one launch (start us, length us, event | category | flops | bytes accessed | tf_op | source)
XLA Modules:
  0.0 189.6 jit_solution(15634337268453216033)
XLA Ops:
  7.2 0.0 copy-start
  7.2 0.0 all-gather.3.cloned.1.call-start
  7.2 0.7 all-gather.3.cloned.1.call-update
  7.9 0.0 all-gather.5.cloned.1.call-start
  8.0 0.7 all-gather.5.cloned.1.call-update
  8.7 27.3 %all_gather.9.lat_ref = bf16[512,768]{1,0:T(8,128)(2,1)S(1)} all-gather(bf16[16,768]{1,0:T(8,128)(2,1)} %param.6), channel_id=1, replica_groups=mesh['seq'=32,'vid'=8] {'seq'}, dimensions={0}, use_global_device_ids=true | all-gather | bytes 811008 | tf_op jit(solution)/shard_map/all_gather | solution.py:257
  35.9 0.0 copy-start.1
  35.9 0.2 fusion.2
  36.2 0.0 copy-done
  36.2 0.4 fusion
  36.6 1.1 fusion.3.lat_ref
  37.7 0.0 copy-done.1
  37.7 1.5 fusion.1.tok_ref
  39.2 28.0 %all-gather.3.cloned.1.call-done = bf16[4,768,768]{2,1,0:T(8,128)(2,1)} async-done(((bf16[4,24,768]{2,1,0:T(8,128)(2,1)}), bf16[4,768,768]{2,1,0:T(8,128)(2,1)}) %all-gather.3.cloned.1.call-update) | async-done | bytes 4718608 | tf_op jit(solution)/shard_map/all_gather | solution.py:255
  67.2 4.0 %slice.8.weight_ref = bf16[3,768,768]{2,1,0:T(8,128)(2,1)} slice(bf16[4,768,768]{2,1,0:T(8,128)(2,1)} %all-gather.3.cloned.1.call-done), slice={[0:3], [0:768], [0:768]} | slice | bytes 7077888 | tf_op jit(solution)/shard_map/slice | solution.py:278
  71.1 20.2 %read.1 = bf16[512,896]{1,0:T(8,128)(2,1)} custom-call(bf16[1024,768]{1,0:T(8,128)(2,1)} %fusion.1.tok_ref, bf16[512,768]{1,0:T(8,128)(2,1)} %fusion.3.lat_ref, bf16[3,768,768]{2,1,0:T(8,128)(2,1)} %slice.8.weight_ref, f32[3,12]{1,0:T(4,128)} %scale_ref.3), custom_call_target="tpu_custom_call" | custom-call | flops 20000000000 | bytes 8000000 | tf_op jit(solution)/shard_map/read/pallas_call | solution.py:261
  91.3 21.7 %all_to_all.16 = bf16[32,16,896]{2,1,0:T(8,128)(2,1)} all-to-all(bf16[32,16,896]{2,1,0:T(8,128)(2,1)} %bitcast.8), channel_id=1, replica_groups=mesh['seq'=32,'vid'=8] {'seq'}, dimensions={0} | all-to-all | bytes 1835008 | tf_op jit(solution)/shard_map/all_to_all | solution.py:279
  113.0 2.9 %combine.1 = bf16[32,16,768]{2,1,0:T(8,128)(2,1)} custom-call(bf16[512,896]{1,0:T(8,128)(2,1)} %bitcast.6), custom_call_target="tpu_custom_call" | custom-call | tf_op jit(solution)/shard_map/combine/pallas_call | solution.py:280
  115.9 5.2 %all-to-all-start.1 = ((bf16[32,16,768]{2,1,0:T(8,128)(2,1)}), bf16[32,16,768]{2,1,0:T(8,128)(2,1)S(1)}, u32[]{:S(2)}, u32[]{:S(2)}) async-start(bf16[32,16,768]{2,1,0:T(8,128)(2,1)} %combine.1), calls=%async_computation.1 | async-start | bytes 1572864 | tf_op jit(solution)/shard_map/all_to_all | solution.py:288
  121.1 2.4 %slice_bitcast_fusion.out_weight_ref = bf16[768,768]{1,0:T(8,128)(2,1)} fusion(bf16[4,768,768]{2,1,0:T(8,128)(2,1)} %all-gather.3.cloned.1.call-done), kind=kLoop, calls=%fused_computation.8 | loop fusion | bytes 2359296 | tf_op jit(solution)/shard_map/squeeze | solution.py:311
  123.5 15.9 %all-to-all-done.1 = bf16[32,16,768]{2,1,0:T(8,128)(2,1)S(1)} async-done(((bf16[32,16,768]{2,1,0:T(8,128)(2,1)}), bf16[32,16,768]{2,1,0:T(8,128)(2,1)S(1)}, u32[]{:S(2)}, u32[]{:S(2)}) %all-to-all-start.1) | async-done | bytes 786464 | tf_op jit(solution)/shard_map/all_to_all | solution.py:288
  139.3 0.0 copy-start.2
  139.3 0.0 all-gather.5.cloned.1.call-done.weight_ref
  139.3 0.9 copy-done.2
  140.2 42.5 %write.1 = (bf16[1024,768]{1,0:T(8,128)(2,1)}, f32[16,768]{1,0:T(8,128)}) custom-call(s32[1]{0:T(128)} %bitcast.index_ref, f32[3,12]{1,0:T(4,128)} %scale_ref.3, bf16[512,768]{1,0:T(8,128)(2,1)} %bitcast.7, bf16[512,768]{1,0:T(8,128)(2,1)} %copy-done.1, bf16[768,768]{1,0:T(8,128)(2,1)} %slice_bitcast_fusion.out_weight_ref, ...), custom_call_target="tpu_custom_call" | custom-call | tf_op jit(solution)/shard_map/write/pallas_call | solution.py:290
  (2 shorter events, 0.0 us)
Async XLA Ops:
  7.2 29.0 %copy-start = (bf16[1024,768]{1,0:T(8,128)(2,1)S(1)}, bf16[1024,768]{1,0:T(8,128)(2,1)}, u32[]{:S(2)}) copy-start(bf16[1024,768]{1,0:T(8,128)(2,1)} %raw_ref.1) | copy-start | bytes 4718596
  7.2 60.0 %all-gather.3.cloned.1.call-start = ((), (), s32[]{:S(2)}) async-start(), calls=%async_computation.2 | async-start | bytes 4866048 | tf_op jit(solution)/shard_map/all_gather | solution.py:255
  7.9 131.4 %all-gather.5.cloned.1.call-start = ((), (), s32[]{:S(2)}) async-start(), calls=%async_computation.3 | async-start | bytes 9732096 | tf_op jit(solution)/shard_map/all_gather | solution.py:256
  35.9 1.7 copy-start.1
  115.9 23.4 %all-to-all-start.1 = ((bf16[32,16,768]{2,1,0:T(8,128)(2,1)}), bf16[32,16,768]{2,1,0:T(8,128)(2,1)S(1)}, u32[]{:S(2)}, u32[]{:S(2)}) async-start(bf16[32,16,768]{2,1,0:T(8,128)(2,1)} %combine.1), calls=%async_computation.1 | async-start | bytes 1572864 | tf_op jit(solution)/shard_map/all_to_all | solution.py:288
  139.3 0.9 copy-start.2
Sparse Core Ops, SparseCore 0:
  10.7 56.4 all-gather.2
  69.8 68.7 all-gather.4

commit v2 on v1

--- a/solution.py
+++ b/solution.py
@@ -19,6 +19,7 @@
 PIECE = 20
 ODD_TOTALS = 12
 EVEN_TOTALS = 64
+CORES = 2
 
 
 def norm_rows(values):
@@ -46,8 +47,10 @@
     low = (squares - high.astype(F32)).astype(BF16)
     parts = []
     for start in range(0, values.shape[1], 256):
-        cols = slice(start, start + 256)
-        mean = dot(high[:, cols], mean_matrix) + dot(low[:, cols], mean_matrix)
+        cols = slice(start, min(start + 256, values.shape[1]))
+        size = cols.stop - start
+        matrix = mean_matrix[:size, :size]
+        mean = dot(high[:, cols], matrix) + dot(low[:, cols], matrix)
         parts.append((values[:, cols] * lax.rsqrt(mean + EPSILON)).astype(BF16))
     return jnp.concatenate(parts, axis=1)
 
@@ -94,9 +97,9 @@
     return top_even, top_odd, dot(exp_even, even), dot(exp_odd, odd)
 
 
-def factors(scale_ref, stage, pair):
+def factors(scale_ref, stage, head):
     root = math.sqrt(HEAD_DIM)
-    return scale_ref[stage, 2 * pair] / root, scale_ref[stage, 2 * pair + 1] / root
+    return scale_ref[stage, head] / root, scale_ref[stage, head + 1] / root
 
 
 def attend(q_ref, k_ref, even_ref, odd_ref, scale_ref, stage, out_ref, block=256):
@@ -111,7 +114,7 @@
             k_ref[:, cols],
             even_ref[:, cols],
             odd_ref[:, cols],
-            *factors(scale_ref, stage, pair),
+            *factors(scale_ref, stage, 2 * pair),
         )
         mask = first_half(even.shape)
         summed = jnp.where(mask, even, odd)
@@ -123,13 +126,31 @@
 
 
 def read_kernel(
-    tok_ref, lat_ref, weight_ref, scale_ref, out_ref, q_ref, k_ref, even_ref, odd_ref, extra_ref
+    core_ref,
+    scale_ref,
+    own_ref,
+    peer_ref,
+    lat_ref,
+    weight_ref,
+    out_ref,
+    q_ref,
+    k_ref,
+    even_ref,
+    odd_ref,
+    extra_ref,
 ):
     mean_matrix = head_mean_matrix()
-    width = tok_ref.shape[1]
-    project_heads(lat_ref, weight_ref.at[0], mean_matrix, q_ref)
-    project_heads(tok_ref, weight_ref.at[1], mean_matrix, k_ref)
-    project_values(tok_ref, weight_ref.at[2], even_ref, odd_ref)
+    width = q_ref.shape[1]
+    heads = width // HEAD_DIM
+    n_tok = own_ref.shape[0]
+    columns = [pl.ds(i * width, width) for i in range(3)]
+    project_heads(lat_ref, weight_ref.at[:, columns[0]], mean_matrix, q_ref)
+    for slab, tok_ref in enumerate((own_ref, peer_ref)):
+        rows = pl.ds(slab * n_tok, n_tok)
+        project_heads(tok_ref, weight_ref.at[:, columns[1]], mean_matrix, k_ref.at[rows, :])
+        project_values(
+            tok_ref, weight_ref.at[:, columns[2]], even_ref.at[rows, :], odd_ref.at[rows, :]
+        )
     extra_ref[...] = jnp.zeros_like(extra_ref)
     block = 256
     n_blocks = lat_ref.shape[0] // block
@@ -138,7 +159,7 @@
         pair, row = i // n_blocks, i % n_blocks
         cols = pl.ds(pl.multiple_of(pair * PAIR, PAIR), PAIR)
         rows = pl.ds(pl.multiple_of(row * block, block), block)
-        even_factor, odd_factor = factors(scale_ref, 0, pair)
+        even_factor, odd_factor = factors(scale_ref, 0, core_ref[0] * heads + 2 * pair)
         top_even, top_odd, even, odd = pair_parts(
             q_ref[rows, cols],
             k_ref[:, cols],
@@ -157,7 +178,7 @@
         extra_ref[rows, :] = extra
         return carry
 
-    lax.fori_loop(0, n_blocks * (HEADS // 2), step, 0)
+    lax.fori_loop(0, n_blocks * (heads // 2), step, 0)
     extra = extra_ref[...]
     high = extra.astype(BF16).astype(F32)
     mid = (extra - high).astype(BF16).astype(F32)
@@ -166,9 +187,9 @@
     out_ref[:, width:] = packed.astype(BF16)
 
 
-def combine_kernel(part_ref, out_ref, *, slabs):
+def combine_kernel(part_ref, out_ref, *, parts):
     width = out_ref.shape[-1]
-    own_rows = out_ref.shape[1]
+    rows = out_ref.shape[1]
     lane = lax.broadcasted_iota(jnp.int32, (PAIR, width), 0)
     head = lax.broadcasted_iota(jnp.int32, (PAIR, width), 1) // HEAD_DIM
     total_lane = jnp.where(head % 2 == 0, EVEN_TOTALS, ODD_TOTALS) + head // 2
@@ -178,7 +199,7 @@
         pick_top = jnp.where(lane == head + piece * PIECE, 1.0, pick_top)
         pick_total = jnp.where(lane == total_lane + piece * PIECE, 1.0, pick_total)
     extra = part_ref[:, width:]
-    shape = (slabs, own_rows, width)
+    shape = (parts, rows, width)
     tops = dot(extra, pick_top.astype(BF16)).reshape(shape)
     totals = dot(extra, pick_total.astype(BF16)).reshape(shape)
     rescale = jnp.exp(tops - jnp.max(tops, axis=0, keepdims=True))
@@ -192,7 +213,6 @@
     scale_ref,
     mix_ref,
     lat_ref,
-    out_weight_ref,
     weight_ref,
     raw_ref,
     tok_ref,
@@ -212,32 +232,40 @@
     n_lat = lat_ref.shape[0]
     own_rows = lat_out_ref.shape[0]
 
-    def first(rows):
-        lat_one = lat_ref[rows, :].astype(F32) + dot(mix_ref[rows, :], out_weight_ref[...])
+    chips, cores, chip_rows, half = mix_ref.shape
+    step = 256 // chip_rows
+
+    def first(chip, carry):
+        rows = pl.ds(pl.multiple_of(chip * 256, 256), 256)
+        lat_one = lat_ref[rows, :].astype(F32)
+        for core in range(cores):
+            mix = mix_ref[pl.ds(chip * step, step), core].reshape(256, half)
+            lat_one += dot(mix, weight_ref[0, core * half : (core + 1) * half, :])
         stream_ref[rows, :] = lat_one
         normed_ref[rows, :] = norm_rows(lat_one).astype(BF16)
-
-    row_blocks(n_lat, 256, first)
-    project_heads(normed_ref, weight_ref.at[0], mean_matrix, q_ref)
-    project_heads(normed_ref, weight_ref.at[1], mean_matrix, k_ref)
-    project_values(normed_ref, weight_ref.at[2], even_ref, odd_ref)
+        return carry
+
+    lax.fori_loop(0, n_lat // 256, first, 0)
+    project_heads(normed_ref, weight_ref.at[1], mean_matrix, q_ref)
+    project_heads(normed_ref, weight_ref.at[2], mean_matrix, k_ref)
+    project_values(normed_ref, weight_ref.at[3], even_ref, odd_ref)
     attend(q_ref, k_ref, even_ref, odd_ref, scale_ref, 1, att_ref)
 
     def second(rows):
-        lat_two = stream_ref[rows, :] + dot(att_ref[rows, :], weight_ref[3])
+        lat_two = stream_ref[rows, :] + dot(att_ref[rows, :], weight_ref[4])
         stream_ref[rows, :] = lat_two
         normed_ref[rows, :] = norm_rows(lat_two).astype(BF16)
 
     row_blocks(n_lat, 256, second)
     own = pl.ds(pl.multiple_of(index_ref[0] * own_rows, own_rows), own_rows)
     lat_out_ref[...] = stream_ref[own, :]
-    project_heads(normed_ref, weight_ref.at[5], mean_matrix, k_ref)
-    project_values(normed_ref, weight_ref.at[6], even_ref, odd_ref)
-    project_heads(tok_ref, weight_ref.at[4], mean_matrix, write_q_ref)
+    project_heads(normed_ref, weight_ref.at[6], mean_matrix, k_ref)
+    project_values(normed_ref, weight_ref.at[7], even_ref, odd_ref)
+    project_heads(tok_ref, weight_ref.at[5], mean_matrix, write_q_ref)
     attend(write_q_ref, k_ref, even_ref, odd_ref, scale_ref, 2, write_att_ref)
 
     def last(rows):
-        update = dot(write_att_ref[rows, :], weight_ref[7])
+        update = dot(write_att_ref[rows, :], weight_ref[8])
         tok_out_ref[rows, :] = (raw_ref[rows, :].astype(F32) + update).astype(BF16)
 
     row_blocks(raw_ref.shape[0], 256, last)
@@ -250,43 +278,63 @@
 def shards(tokens, latents, read_weights, later_weights, head_scale):
     n_tok, width = tokens.shape
     own_rows = latents.shape[0]
-    slabs = lax.axis_size("seq")
-    n_lat = own_rows * slabs
-    read_full = lax.all_gather(read_weights, "seq", axis=1, tiled=True)
-    later_full = lax.all_gather(later_weights, "seq", axis=1, tiled=True)
+    devices = lax.axis_size("seq")
+    chips = devices // CORES
+    n_lat = own_rows * devices
+    half = width // CORES
+    weight_rows = read_weights.shape[1]
+    index = lax.axis_index("seq").astype(jnp.int32)
+    same_core = [[CORES * chip + core for chip in range(chips)] for core in range(CORES)]
+    swap = [(device, device ^ 1) for device in range(devices)]
+
+    first = read_weights[:3].reshape(3, weight_rows, CORES, half).transpose(2, 1, 0, 3)
+    first = first.reshape(1, CORES, weight_rows, 3 * half)
+    first = jnp.broadcast_to(first, (chips,) + first.shape[1:])
+    first = first.reshape(devices, weight_rows, 3 * half)
+    first = lax.all_to_all(first, "seq", 0, 0, tiled=True).reshape(width, 3 * half)
+    rest = jnp.concatenate([read_weights[3:], later_weights])
+    rest = lax.all_gather(rest, "seq", axis=1, tiled=True)
     lat_full = lax.all_gather(latents, "seq", axis=0, tiled=True)
     tok_normed = norm_rows(tokens).astype(BF16)
+    peer_normed = lax.ppermute(tok_normed, "seq", swap)
     lat_normed = norm_rows(lat_full).astype(BF16)
     params = pltpu.CompilerParams(vmem_limit_bytes=VMEM_LIMIT)
     parts = pl.pallas_call(
         read_kernel,
         name="read",
-        out_shape=jax.ShapeDtypeStruct((n_lat, width + PAIR), BF16),
-        in_specs=[IN_VMEM, IN_VMEM, IN_VMEM, IN_SMEM],
+        out_shape=jax.ShapeDtypeStruct((n_lat, half + PAIR), BF16),
+        in_specs=[IN_SMEM, IN_SMEM] + [IN_VMEM] * 4,
         out_specs=IN_VMEM,
         scratch_shapes=[
-            pltpu.VMEM((n_lat, width), BF16),
-            pltpu.VMEM((n_tok, width), BF16),
-            pltpu.VMEM((n_tok, width), BF16),
-            pltpu.VMEM((n_tok, width), BF16),
+            pltpu.VMEM((n_lat, half), BF16),
+            pltpu.VMEM((2 * n_tok, half), BF16),
+            pltpu.VMEM((2 * n_tok, half), BF16),
+            pltpu.VMEM((2 * n_tok, half), BF16),
             pltpu.VMEM((n_lat, PAIR), F32),
         ],
         compiler_params=params,
         cost_estimate=pl.CostEstimate(
             flops=20_000_000_000, bytes_accessed=8_000_000, transcendentals=6_300_000
         ),
-    )(tok_normed, lat_normed, read_full[:3], head_scale)
-    parts = lax.all_to_all(parts, "seq", 0, 0, tiled=True)
+    )((index % CORES).reshape(1), head_scale, tok_normed, peer_normed, lat_normed, first)
+    parts = lax.all_to_all(
+        parts.reshape(chips, CORES * own_rows, half + PAIR),
+        "seq",
+        0,
+        0,
+        tiled=True,
+        axis_index_groups=same_core,
+    )
     mixed = pl.pallas_call(
-        functools.partial(combine_kernel, slabs=slabs),
+        functools.partial(combine_kernel, parts=chips),
         name="combine",
-        out_shape=jax.ShapeDtypeStruct((slabs, own_rows, width), BF16),
+        out_shape=jax.ShapeDtypeStruct((devices, CORES * own_rows, half), BF16),
         in_specs=[IN_VMEM],
         out_specs=IN_VMEM,
         compiler_params=params,
-    )(parts)
-    mixed = lax.all_to_all(mixed, "seq", 0, 0, tiled=True).reshape(n_lat, width)
-    index = lax.axis_index("seq").astype(jnp.int32).reshape(1)
+    )(parts.reshape(n_lat, half + PAIR))
+    mixed = lax.all_to_all(mixed, "seq", 0, 0, tiled=True)
+    mixed = mixed.reshape(chips, CORES, CORES * own_rows, half)
     return pl.pallas_call(
         write_kernel,
         name="write",
@@ -294,7 +342,7 @@
             jax.ShapeDtypeStruct(tokens.shape, BF16),
             jax.ShapeDtypeStruct(latents.shape, F32),
         ),
-        in_specs=[IN_SMEM, IN_SMEM] + [IN_VMEM] * 6,
+        in_specs=[IN_SMEM, IN_SMEM] + [IN_VMEM] * 5,
         out_specs=(IN_VMEM, IN_VMEM),
         scratch_shapes=[
             pltpu.VMEM((n_lat, width), F32),
@@ -308,7 +356,7 @@
             pltpu.VMEM((n_tok, width), BF16),
         ],
         compiler_params=params,
-    )(index, head_scale, mixed, lat_full, read_full[3], later_full, tokens, tok_normed)
+    )(index.reshape(1), head_scale, mixed, lat_full, rest, tokens, tok_normed)
 
 
 def solution(mesh):

time: 190 us -> 178 us (0.937)
  waiting for transfers between devices: 45.2 us -> 0.02 us
  blocking collectives: 49 us -> 80.4 us
  starting transfers between devices: 5.25 us -> 9.19 us
  local copies, waits for them, and re-layouts: 7.22 us -> 3.29 us
    all_gather x2 -> x1, waiting for transfers between devices: 28 us -> 0.01 us  [shards(): rest = lax.all_gather(rest, 'seq', axis=1, tiled=True)]
    all_gather x1, blocking collectives: 27.3 us -> 44.8 us  [shards(): lat_full = lax.all_gather(latents, 'seq', axis=0, tiled=True)]
    all_to_all x1, waiting for transfers between devices: 15.9 us -> 0.01 us  [shards(): lax.all_to_all(first, 'seq', 0, 0, tiled=True).reshape(width, 3 * half)]
    all_to_all x1 -> x2, blocking collectives: 21.7 us -> 35.6 us  [the longest x1 20.8 us: shards(): mixed = lax.all_to_all(mixed, 'seq', 0, 0, tiled=True)]
    all_to_all x1, starting transfers between devices: 5.18 us -> 8.77 us  [shards(): lax.all_to_all(first, 'seq', 0, 0, tiled=True).reshape(width, 3 * half)]
    squeeze x1 -> x0, local copies, waits for them, and re-layouts: 2.36 us -> none  [shards(): read_full[3]]
    slice x1 -> x2, local copies, waits for them, and re-layouts: 3.96 us -> 1.68 us  [the longest x1 0.91 us: shards(): read_weights[:3].reshape(3, weight_rows, CORES, half).transpose(2, 1, 0, 3)]
  transfers between devices with their start and end apart: 3 -> 3, of which waited for: 2 -> 0; matrix products, arithmetic and copies ran while one was open for 5% -> 3% of each run, Pallas kernels for 12% -> 13%
where the time goes in v2:
time: 178 us; the launch traced here: 177 us
  blocking collectives  80.4 us (45%)
  Pallas kernels  66.3 us (37%)
  between operations  14.1 us (8%)
  starting transfers between devices  9.19 us (5%)
  other arithmetic  3.75 us (2%)
  local copies, waits for them, and re-layouts  3.29 us (2%)
    all_gather x1, blocking collectives, shards(): lat_full = lax.all_gather(latents, 'seq', axis=0, tiled=True)  44.8 us
    pallas_call x1, Pallas kernels, shards(): pl.pallas_call(write_kernel, name='write', out_shape=(jax.ShapeDtypeStruc...  42.7 us
    pallas_call x1, Pallas kernels, shards(): pl.pallas_call(read_kernel, name='read', out_shape=jax.ShapeDtypeStruct((...  21.1 us
    all_to_all x1, blocking collectives, shards(): mixed = lax.all_to_all(mixed, 'seq', 0, 0, tiled=True)  20.8 us
    all_to_all x1, blocking collectives, shards(): lax.all_to_all(parts.reshape(chips, CORES * own_rows, half + PAIR), 'seq'...  14.8 us
    all_to_all x1, starting transfers between devices, shards(): lax.all_to_all(first, 'seq', 0, 0, tiled=True).reshape(width, 3 * half)  8.77 us
  transfers between devices with their start and end apart: 3, of which 0 were waited for; matrix products, arithmetic and copies ran while one was open for 3% of the time, Pallas kernels for 13%

profile of v2, /device:TPU:1, one launch (start us, length us, event | category | flops | bytes accessed | tf_op | source)
XLA Modules:
  0.0 177.1 jit_solution(8848643140838278813)
XLA Ops:
  7.2 0.0 all-gather.2.cloned.1.call-start
  7.2 0.8 slice.7
  8.0 1.7 pad_maximum_fusion
  9.7 0.0 all-gather.2.cloned.1.call-update
  9.7 0.9 slice.6
  10.7 0.1 copy.9
  10.7 0.1 broadcast_in_dim.4
  10.8 1.4 broadcast_in_dim.10
  12.3 0.0 copy-start
  12.3 8.8 %all-to-all-start = ((bf16[32,24,1152]{2,1,0:T(8,128)(2,1)}), bf16[32,24,1152]{2,1,0:T(8,128)(2,1)}, u32[]{:S(2)}, u32[]{:S(2)}) async-start(bf16[32,24,1152]{2,1,0:T(8,128)(2,1)} %bitcast.3), calls=%async_computation | async-start | bytes 3538944 | tf_op jit(solution)/shard_map/all_to_all | solution.py:294
  21.0 0.0 copy-done
  21.0 0.4 fusion
  21.4 0.0 copy-start.3
  21.4 0.3 fusion.1.own_ref.tok_ref
  21.8 0.0 copy-start.2
  21.8 0.4 collective-permute-start
  22.2 0.0 copy-done.3
  22.2 44.8 %all_gather.6.lat_ref = bf16[512,768]{1,0:T(8,128)(2,1)S(1)} all-gather(bf16[16,768]{1,0:T(8,128)(2,1)S(1)} %copy-done.3), channel_id=1, replica_groups=mesh['seq'=32,'vid'=8] {'seq'}, dimensions={0}, use_global_device_ids=true | all-gather | bytes 811008 | tf_op jit(solution)/shard_map/all_gather | solution.py:297
  67.0 0.0 copy-start.1
  67.0 0.2 fusion.2
  67.2 1.1 fusion.3.lat_ref
  68.3 0.0 copy-done.2
  68.3 0.0 collective-permute-done.peer_ref
  68.3 0.0 all-to-all-done
  68.3 21.1 %read.1 = bf16[512,512]{1,0:T(8,128)(2,1)} custom-call(s32[1]{0:T(128)} %bitcast.1.core_ref, f32[3,12]{1,0:T(4,128)} %scale_ref.3, bf16[1024,768]{1,0:T(8,128)(2,1)} %copy-done.2, bf16[1024,768]{1,0:T(8,128)(2,1)} %collective-permute-done.peer_ref, bf16[512,768]{1,0:T(8,128)(2,1)} %fusion.3.lat_ref, bf16[768,1152]{1,0:T(8,128)(2,1)} %bitcast.4.weight_ref), custom_call_target="tpu_custom_call" | custom-call | flops 20000000000 | bytes 8000000 | tf_op jit(solution)/shard_map/read/pallas_call | solution.py:302
  89.4 0.0 copy-done.1
  89.4 14.8 %all_to_all.15 = bf16[16,32,512]{2,1,0:T(8,128)(2,1)} all-to-all(bf16[16,32,512]{2,1,0:T(8,128)(2,1)} %bitcast.13), channel_id=1, replica_groups={{0,16,32,48,64,80,96,112,128,144,160,176,192,208,224,240},{8,24,40,56,7..., dimensions={0} | all-to-all | bytes 1048576 | tf_op jit(solution)/shard_map/all_to_all | solution.py:320
  104.2 2.4 %combine.1 = bf16[32,32,384]{2,1,0:T(8,128)(2,1)} custom-call(bf16[512,512]{1,0:T(8,128)(2,1)} %bitcast.11), custom_call_target="tpu_custom_call" | custom-call | tf_op jit(solution)/shard_map/combine/pallas_call | solution.py:328
  106.6 20.8 %all_to_all.16 = bf16[32,32,384]{2,1,0:T(8,128)(2,1)} all-to-all(bf16[32,32,384]{2,1,0:T(8,128)(2,1)} %combine.1), channel_id=1, replica_groups=mesh['seq'=32,'vid'=8] {'seq'}, dimensions={0} | all-to-all | bytes 1572864 | tf_op jit(solution)/shard_map/all_to_all | solution.py:336
  127.5 0.0 all-gather.2.cloned.1.call-done.weight_ref
  127.5 42.7 %write.1 = (bf16[1024,768]{1,0:T(8,128)(2,1)}, f32[16,768]{1,0:T(8,128)}) custom-call(s32[1]{0:T(128)} %bitcast.index_ref, f32[3,12]{1,0:T(4,128)} %scale_ref.3, bf16[16,2,32,384]{3,2,1,0:T(8,128)(2,1)} %bitcast.10, bf16[512,768]{1,0:T(8,128)(2,1)} %copy-done.1, bf16[9,768,768]{2,1,0:T(8,128)(2,1)} %all-gather.2.cloned.1.call-done.weight_ref, ...), custom_call_target="tpu_custom_call" | custom-call | tf_op jit(solution)/shard_map/write/pallas_call | solution.py:338
  (3 shorter events, 0.0 us)
Async XLA Ops:
  7.2 120.3 %all-gather.2.cloned.1.call-start = ((), (), s32[]{:S(2)}) async-start(), calls=%async_computation.3 | async-start | bytes 10948608 | tf_op jit(solution)/shard_map/all_gather | solution.py:296
  12.3 8.8 %copy-start = (bf16[1024,768]{1,0:T(8,128)(2,1)S(1)}, bf16[1024,768]{1,0:T(8,128)(2,1)}, u32[]{:S(2)}) copy-start(bf16[1024,768]{1,0:T(8,128)(2,1)} %raw_ref.1) | copy-start | bytes 4718596
  12.3 56.0 %all-to-all-start = ((bf16[32,24,1152]{2,1,0:T(8,128)(2,1)}), bf16[32,24,1152]{2,1,0:T(8,128)(2,1)}, u32[]{:S(2)}, u32[]{:S(2)}) async-start(bf16[32,24,1152]{2,1,0:T(8,128)(2,1)} %bitcast.3), calls=%async_computation | async-start | bytes 3538944 | tf_op jit(solution)/shard_map/all_to_all | solution.py:294
  21.4 0.7 copy-start.3
  21.8 46.5 %copy-start.2 = (bf16[1024,768]{1,0:T(8,128)(2,1)}, bf16[1024,768]{1,0:T(8,128)(2,1)S(1)}, u32[]{:S(2)}) copy-start(bf16[1024,768]{1,0:T(8,128)(2,1)S(1)} %fusion.1.own_ref.tok_ref) | copy-start | bytes 4718596
  21.8 46.5 %collective-permute-start = (bf16[1024,768]{1,0:T(8,128)(2,1)S(1)}, bf16[1024,768]{1,0:T(8,128)(2,1)}, u32[]{:S(2)}, u32[]{:S(2)}) collective-permute-start(bf16[1024,768]{1,0:T(8,128)(2,1)S(1)} %fusion.1.own_ref.tok_ref), channel_id=1, source_target_pairs={{0,8},{8,0},{16,24},{24,16},{32,40},{40,32},{48,56},{56,48},{64,72... | collective-permute-start | bytes 4718600 | tf_op jit(solution)/shard_map/ppermute | solution.py:299
  67.0 22.4 %copy-start.1 = (bf16[512,768]{1,0:T(8,128)(2,1)}, bf16[512,768]{1,0:T(8,128)(2,1)S(1)}, u32[]{:S(2)}) copy-start(bf16[512,768]{1,0:T(8,128)(2,1)S(1)} %all_gather.6.lat_ref) | copy-start | bytes 2359300
Sparse Core Ops, SparseCore 0:
  10.7 78.1 all-gather.1

commit v3 on v2

v3 whole, which is shorter than its diff:
```python
import functools
import math

import jax
import jax.numpy as jnp
from jax import lax
from jax.experimental import pallas as pl
from jax.experimental.pallas import tpu as pltpu
from jax.sharding import PartitionSpec as P

HEADS = 12
HEAD_DIM = 64
PAIR = 2 * HEAD_DIM
EPSILON = 1e-06
LOG2E = math.log2(math.e)
BF16 = jnp.bfloat16
F32 = jnp.float32
VMEM_LIMIT = 56 * 1024 * 1024
PIECE = 16
TOTALS = 6
CORES = 2


def norm_rows(values):
    values = values.astype(F32)
    return values * lax.rsqrt(jnp.mean(values * values, axis=-1, keepdims=True) + EPSILON)


def dot(left, right):
    return jnp.dot(left, right, preferred_element_type=F32)


def dot_nt(left, right):
    return lax.dot_general(left, right, (((1,), (1,)), ((), ())), preferred_element_type=F32)


def head_mean_matrix():
    rows = lax.broadcasted_iota(jnp.int32, (256, 256), 0) // HEAD_DIM
    cols = lax.broadcasted_iota(jnp.int32, (256, 256), 1) // HEAD_DIM
    return jnp.where(rows == cols, 1.0 / HEAD_DIM, 0.0).astype(BF16)


def head_norm(values, mean_matrix):
    squares = values * values
    high = squares.astype(BF16)
    low = (squares - high.astype(F32)).astype(BF16)
    parts = []
    for start in range(0, values.shape[1], 256):
        cols = slice(start, min(start + 256, values.shape[1]))
        size = cols.stop - start
        matrix = mean_matrix[:size, :size]
        mean = dot(high[:, cols], matrix) + dot(low[:, cols], matrix)
        parts.append((values[:, cols] * lax.rsqrt(mean + EPSILON)).astype(BF16))
    return jnp.concatenate(parts, axis=1)


def first_half(shape):
    return lax.broadcasted_iota(jnp.int32, shape, 1) % PAIR < HEAD_DIM


def row_blocks(n_rows, block, body):
    def step(i, carry):
        body(pl.ds(pl.multiple_of(i * block, block), block))
        return carry

    lax.fori_loop(0, n_rows // block, step, 0)


def project_heads(x_ref, weight, mean_matrix, out_ref, block=512):
    def body(rows):
        out_ref[rows, :] = head_norm(dot(x_ref[rows, :], weight[...]), mean_matrix)

    row_blocks(x_ref.shape[0], block, body)


def project_values(x_ref, weight, out_ref, block=512):
    def body(rows):
        out_ref[rows, :] = dot(x_ref[rows, :], weight[...]).astype(BF16)

    row_blocks(x_ref.shape[0], block, body)


def attend(q_ref, k_ref, v_ref, factor, emit, block=512, unroll=1):
    n_blocks = q_ref.shape[0] // block
    n_steps = n_blocks * (q_ref.shape[1] // PAIR)

    def step(i, carry):
        pair, row = i // n_blocks, i % n_blocks
        cols = pl.ds(pl.multiple_of(pair * PAIR, PAIR), PAIR)
        rows = pl.ds(pl.multiple_of(row * block, block), block)
        queries, keys, values = q_ref[rows, cols], k_ref[:, cols], v_ref[:, cols]
        values = jnp.concatenate([values, jnp.ones_like(values)], axis=1)
        mask = first_half(queries.shape)
        zero = jnp.zeros_like(queries)
        heads = []
        for which in range(2):
            own = (mask, queries, zero) if which == 0 else (mask, zero, queries)
            scores = dot_nt(jnp.where(*own), keys)
            top = jnp.max(scores, axis=1, keepdims=True)
            weights = jnp.exp2((scores - top) * (factor(2 * pair + which) * LOG2E))
            both = dot(weights.astype(BF16), values)
            heads.append((top, both[:, :PAIR], both[:, PAIR:]))
        emit(pair, rows, cols, heads)
        return carry

    lax.fori_loop(0, n_steps, step, 0, unroll=unroll)


def attend_into(q_ref, k_ref, v_ref, scale_ref, stage, out_ref, unroll):
    def emit(pair, rows, cols, heads):
        (_, even, even_total), (_, odd, odd_total) = heads
        mask = first_half(even.shape)
        total = jnp.where(mask, even_total, odd_total)
        inverse = pl.reciprocal(total, approx=True)
        inverse = inverse * (2.0 - total * inverse)
        out_ref[rows, cols] = (jnp.where(mask, even, odd) * inverse).astype(BF16)

    def factor(head):
        return scale_ref[stage, head] / math.sqrt(HEAD_DIM)

    attend(q_ref, k_ref, v_ref, factor, emit, unroll=unroll)


def pack_kernel(read_ref, later_ref, lat_ref, first_ref, rest_ref):
    _, n_rows, width = read_ref.shape
    own_rows = lat_ref.shape[0]
    half = width // CORES
    rest_ref[0] = read_ref[3]
    rest_ref[1:] = later_ref[...]
    lat = lat_ref[...].astype(F32)
    split = own_rows * width // n_rows
    low = own_rows // 2
    extra = jnp.concatenate([lat[:low, split:], lat[low:, split:]], axis=1)
    extra = jnp.concatenate([lat[:, :split], extra], axis=0).astype(BF16)
    for core in range(CORES):
        cols = slice(core * half, (core + 1) * half)
        block = jnp.concatenate([read_ref[i][:, cols] for i in range(3)] + [extra], axis=1)
        first_ref[:, core] = jnp.broadcast_to(block[None], (first_ref.shape[0],) + block.shape)


def unpack_latents(first, own_rows, width):
    devices, n_rows, _ = first.shape
    split = own_rows * width // n_rows
    first = first[:, :, -split:]
    low = first[:, own_rows:]
    low = jnp.concatenate([low[:, :, : split // 2], low[:, :, split // 2 :]], axis=1)
    return jnp.concatenate([first[:, :own_rows], low], axis=2).reshape(devices * own_rows, width)


def read_kernel(
    core_ref,
    scale_ref,
    own_ref,
    peer_ref,
    lat_ref,
    weight_ref,
    out_ref,
    q_ref,
    k_ref,
    v_ref,
    extra_ref,
):
    mean_matrix = head_mean_matrix()
    width = q_ref.shape[1]
    n_heads = width // HEAD_DIM
    n_tok = own_ref.shape[0]
    columns = [pl.ds(i * width, width) for i in range(3)]
    project_heads(lat_ref, weight_ref.at[:, columns[0]], mean_matrix, q_ref)
    for slab, tok_ref in enumerate((own_ref, peer_ref)):
        rows = pl.ds(slab * n_tok, n_tok)
        project_heads(tok_ref, weight_ref.at[:, columns[1]], mean_matrix, k_ref.at[rows, :])
        project_values(tok_ref, weight_ref.at[:, columns[2]], v_ref.at[rows, :])
    extra_ref[...] = jnp.zeros_like(extra_ref)

    def factor(head):
        return scale_ref[0, core_ref[0] * n_heads + head] / math.sqrt(HEAD_DIM)

    def emit(pair, rows, cols, heads):
        (_, even, _), (_, odd, _) = heads
        out_ref[rows, cols] = jnp.where(first_half(even.shape), even, odd).astype(BF16)
        lane = lax.broadcasted_iota(jnp.int32, even.shape, 1)
        extra = extra_ref[rows, :]
        for which, (top, _, total) in enumerate(heads):
            head = 2 * pair + which
            extra = jnp.where(lane == head, top * factor(head), extra)
            extra = jnp.where(lane == TOTALS + head, total, extra)
        extra_ref[rows, :] = extra

    attend(q_ref, k_ref, v_ref, factor, emit, unroll=3)
    extra = extra_ref[...]
    high = extra.astype(BF16).astype(F32)
    mid = (extra - high).astype(BF16).astype(F32)
    low = extra - high - mid
    packed = high + pltpu.roll(mid, PIECE, 1) + pltpu.roll(low, 2 * PIECE, 1)
    out_ref[:, width:] = packed.astype(BF16)


def combine_kernel(part_ref, out_ref, *, parts):
    width = out_ref.shape[-1]
    rows = out_ref.shape[1]
    lane = lax.broadcasted_iota(jnp.int32, (PAIR, width), 0)
    head = lax.broadcasted_iota(jnp.int32, (PAIR, width), 1) // HEAD_DIM
    pick_top = jnp.zeros((PAIR, width), F32)
    pick_total = jnp.zeros((PAIR, width), F32)
    for piece in range(3):
        pick_top = jnp.where(lane == head + piece * PIECE, 1.0, pick_top)
        pick_total = jnp.where(lane == head + TOTALS + piece * PIECE, 1.0, pick_total)
    extra = part_ref[:, width:]
    shape = (parts, rows, width)
    tops = dot(extra, pick_top.astype(BF16)).reshape(shape)
    totals = dot(extra, pick_total.astype(BF16)).reshape(shape)
    rescale = jnp.exp(tops - jnp.max(tops, axis=0, keepdims=True))
    sums = part_ref[:, :width].astype(F32).reshape(shape)
    mixed = jnp.sum(rescale * sums, axis=0) / jnp.sum(rescale * totals, axis=0)
    out_ref[...] = jnp.broadcast_to(mixed.astype(BF16)[None], out_ref.shape)


def query_kernel(tok_ref, weight_ref, out_ref):
    project_heads(tok_ref, weight_ref.at[0], head_mean_matrix(), out_ref)


READ_OUT, SELF_Q, SELF_K, SELF_V, SELF_OUT, WRITE_Q, WRITE_K, WRITE_V, WRITE_OUT = range(9)


def write_kernel(
    index_ref,
    scale_ref,
    mix_ref,
    lat_ref,
    weights_ref,
    raw_hbm_ref,
    query_hbm_ref,
    tok_out_ref,
    lat_out_ref,
    weight_ref,
    raw_ref,
    write_q_ref,
    stream_ref,
    normed_ref,
    q_ref,
    k_ref,
    v_ref,
    att_ref,
    write_att_ref,
    sems,
):
    order = (READ_OUT, SELF_Q, SELF_K, SELF_V, SELF_OUT, WRITE_K, WRITE_V, WRITE_OUT)
    copies = {}
    for slot, matrix in enumerate(order):
        copies[matrix] = pltpu.make_async_copy(
            weights_ref.at[matrix], weight_ref.at[slot], sems.at[slot]
        )
    query_copy = pltpu.make_async_copy(query_hbm_ref, write_q_ref, sems.at[len(order)])
    raw_copy = pltpu.make_async_copy(raw_hbm_ref, raw_ref, sems.at[len(order) + 1])
    for matrix in order:
        copies[matrix].start()
    query_copy.start()
    raw_copy.start()

    def ready(matrix):
        copies[matrix].wait()
        return weight_ref.at[order.index(matrix)]

    mean_matrix = head_mean_matrix()
    n_lat = lat_ref.shape[0]
    own_rows = lat_out_ref.shape[0]
    chips, cores, chip_rows, half = mix_ref.shape
    weight = ready(READ_OUT)
    lat_one = lat_ref[...].astype(F32)
    for core in range(cores):
        mix = mix_ref[:, core].reshape(chips * chip_rows, half)
        lat_one += dot(mix, weight[core * half : (core + 1) * half, :])
    stream_ref[...] = lat_one
    normed_ref[...] = norm_rows(lat_one).astype(BF16)
    project_heads(normed_ref, ready(SELF_Q), mean_matrix, q_ref)
    project_heads(normed_ref, ready(SELF_K), mean_matrix, k_ref)
    project_values(normed_ref, ready(SELF_V), v_ref)
    attend_into(q_ref, k_ref, v_ref, scale_ref, 1, att_ref, 6)
    lat_two = stream_ref[...] + dot(att_ref[...], ready(SELF_OUT)[...])
    stream_ref[...] = lat_two
    normed_ref[...] = norm_rows(lat_two).astype(BF16)
    own = pl.ds(pl.multiple_of(index_ref[0] * own_rows, own_rows), own_rows)
    lat_out_ref[...] = stream_ref[own, :]
    project_heads(normed_ref, ready(WRITE_K), mean_matrix, k_ref)
    project_values(normed_ref, ready(WRITE_V), v_ref)
    query_copy.wait()
    attend_into(write_q_ref, k_ref, v_ref, scale_ref, 2, write_att_ref, 4)
    weight = ready(WRITE_OUT)
    raw_copy.wait()

    def last(rows):
        update = dot(write_att_ref[rows, :], weight[...])
        tok_out_ref[rows, :] = (raw_ref[rows, :].astype(F32) + update).astype(BF16)

    row_blocks(raw_ref.shape[0], 512, last)


IN_VMEM = pl.BlockSpec(memory_space=pltpu.VMEM)
IN_SMEM = pl.BlockSpec(memory_space=pltpu.SMEM)
IN_PLACE = pl.BlockSpec(memory_space=pl.ANY)


def shards(tokens, latents, read_weights, later_weights, head_scale):
    n_tok, width = tokens.shape
    own_rows = latents.shape[0]
    devices = lax.axis_size("seq")
    chips = devices // CORES
    n_lat = own_rows * devices
    half = width // CORES
    weight_rows = read_weights.shape[1]
    index = lax.axis_index("seq").astype(jnp.int32)
    same_core = [[CORES * chip + core for chip in range(chips)] for core in range(CORES)]
    swap = [(device, device ^ 1) for device in range(devices)]

    params = pltpu.CompilerParams(vmem_limit_bytes=VMEM_LIMIT)
    packed_width = 3 * half + own_rows * width // weight_rows
    first, rest = pl.pallas_call(
        pack_kernel,
        name="pack",
        out_shape=(
            jax.ShapeDtypeStruct((chips, CORES, weight_rows, packed_width), BF16),
            jax.ShapeDtypeStruct((9, weight_rows, width), BF16),
        ),
        in_specs=[IN_VMEM] * 3,
        out_specs=(IN_VMEM, IN_VMEM),
        compiler_params=params,
    )(read_weights, later_weights, latents)
    first = first.reshape(devices, weight_rows, packed_width)
    first = lax.all_to_all(first, "seq", 0, 0, tiled=True)
    lat_full = unpack_latents(first, own_rows, width)
    first = first.reshape(width, packed_width)
    rest = lax.all_gather(rest, "seq", axis=1, tiled=True)
    tok_normed = norm_rows(tokens).astype(BF16)
    peer_normed = lax.ppermute(tok_normed, "seq", swap)
    lat_normed = norm_rows(lat_full).astype(BF16)
    parts = pl.pallas_call(
        read_kernel,
        name="read",
        out_shape=jax.ShapeDtypeStruct((n_lat, half + PAIR), BF16),
        in_specs=[IN_SMEM, IN_SMEM] + [IN_VMEM] * 4,
        out_specs=IN_VMEM,
        scratch_shapes=[
            pltpu.VMEM((n_lat, half), BF16),
            pltpu.VMEM((2 * n_tok, half), BF16),
            pltpu.VMEM((2 * n_tok, half), BF16),
            pltpu.VMEM((n_lat, PAIR), F32),
        ],
        compiler_params=params,
        cost_estimate=pl.CostEstimate(
            flops=20_000_000_000, bytes_accessed=8_000_000, transcendentals=6_300_000
        ),
    )((index % CORES).reshape(1), head_scale, tok_normed, peer_normed, lat_normed, first)
    queries = pl.pallas_call(
        query_kernel,
        name="query",
        grid=(1,),
        out_shape=jax.ShapeDtypeStruct((n_tok, width), BF16),
        in_specs=[
            pl.BlockSpec((n_tok, width), lambda i: (0, 0)),
            pl.BlockSpec((1, width, width), lambda i: (WRITE_Q, 0, 0)),
        ],
        out_specs=pl.BlockSpec((n_tok, width), lambda i: (0, 0)),
        compiler_params=params,
        cost_estimate=pl.CostEstimate(
            flops=4_000_000_000, bytes_accessed=5_000_000, transcendentals=800_000
        ),
    )(tok_normed, rest)
    parts = lax.all_to_all(
        parts.reshape(chips, CORES * own_rows, half + PAIR),
        "seq",
        0,
        0,
        tiled=True,
        axis_index_groups=same_core,
    )
    mixed = pl.pallas_call(
        functools.partial(combine_kernel, parts=chips),
        name="combine",
        out_shape=jax.ShapeDtypeStruct((devices, CORES * own_rows, half), BF16),
        in_specs=[IN_VMEM],
        out_specs=IN_VMEM,
        compiler_params=params,
    )(parts.reshape(n_lat, half + PAIR))
    mixed = lax.all_to_all(mixed, "seq", 0, 0, tiled=True)
    mixed = mixed.reshape(chips, CORES, CORES * own_rows, half)
    latents_bf16 = pltpu.VMEM((n_lat, width), BF16)
    tokens_bf16 = pltpu.VMEM((n_tok, width), BF16)
    return pl.pallas_call(
        write_kernel,
        name="write",
        out_shape=(
            jax.ShapeDtypeStruct(tokens.shape, BF16),
            jax.ShapeDtypeStruct(latents.shape, F32),
        ),
        in_specs=[IN_SMEM, IN_SMEM, IN_VMEM, IN_VMEM, IN_PLACE, IN_PLACE, IN_PLACE],
        out_specs=(IN_VMEM, IN_VMEM),
        scratch_shapes=[
            pltpu.VMEM((8, width, width), BF16),
            tokens_bf16,
            tokens_bf16,
            pltpu.VMEM((n_lat, width), F32),
            latents_bf16,
            latents_bf16,
            latents_bf16,
            latents_bf16,
            latents_bf16,
            tokens_bf16,
            pltpu.SemaphoreType.DMA((10,)),
        ],
        compiler_params=params,
    )(index.reshape(1), head_scale, mixed, lat_full, rest, tokens, queries)


def solution(mesh):
    placed = (
        P(("vid", "seq"), None),
        P(("vid", "seq"), None),
        P(None, "seq", None),
        P(None, "seq", None),
        P(),
    )
    return jax.shard_map(
        shards,
        mesh=mesh,
        in_specs=placed,
        out_specs=(P(("vid", "seq"), None), P(("vid", "seq"), None)),
        check_vma=False,
    )
```

time: 178 us -> 156 us (0.88)
  blocking collectives: 80.4 us -> 18.9 us
  waiting for transfers between devices: 0.02 us -> 45.4 us
  Pallas kernels: 66.3 us -> 55.9 us
  starting transfers between devices: 9.19 us -> 16.2 us
    all_to_all x1 -> x2, waiting for transfers between devices: 0.01 us -> 45.4 us  [the longest x1 36.5 us: shards(): first = lax.all_to_all(first, 'seq', 0, 0, tiled=True)]
    all_gather x1 -> x0, blocking collectives: 44.8 us -> none  [shards(): lat_full = lax.all_gather(latents, 'seq', axis=0, tiled=True)]
    all_to_all x1 -> x0, blocking collectives: 20.8 us -> none  [shards(): mixed = lax.all_to_all(mixed, 'seq', 0, 0, tiled=True)]
    pallas_call x1, Pallas kernels: 42.7 us -> 27.1 us  [shards(): pl.pallas_call(write_kernel, name='write', out_shape=(jax.ShapeDtypeStruc...]
    pallas_call x0 -> x2, Pallas kernels: none -> 7.96 us  [the longest x1 5.33 us: shards(): pl.pallas_call(query_kernel, name='query', grid=(1,), out_shape=jax.Shape...]
    all_to_all x1 -> x2, starting transfers between devices: 8.77 us -> 15.7 us  [the longest x1 8.78 us: shards(): first = lax.all_to_all(first, 'seq', 0, 0, tiled=True)]
    all_to_all x1, blocking collectives: 14.8 us -> 18.9 us  [shards(): lax.all_to_all(parts.reshape(chips, CORES * own_rows, half + PAIR), 'seq'...]
    pallas_call x1, Pallas kernels: 21.1 us -> 18.3 us  [shards(): pl.pallas_call(read_kernel, name='read', out_shape=jax.ShapeDtypeStruct((...]
  transfers between devices with their start and end apart: 3 -> 4, of which waited for: 0 -> 2; matrix products, arithmetic and copies ran while one was open for 3% -> 3% of each run, Pallas kernels for 13% -> 17%
where the time goes in v3:
time: 156 us
  Pallas kernels  55.9 us (36%)
  waiting for transfers between devices  45.4 us (29%)
  blocking collectives  18.9 us (12%)
  starting transfers between devices  16.2 us (10%)
  between operations  14.1 us (9%)
  local copies, waits for them, and re-layouts  3.08 us (2%)
  other arithmetic  2.05 us (1%)
    all_to_all x1, waiting for transfers between devices, shards(): first = lax.all_to_all(first, 'seq', 0, 0, tiled=True)  36.5 us
    pallas_call x1, Pallas kernels, shards(): pl.pallas_call(write_kernel, name='write', out_shape=(jax.ShapeDtypeStruc...  27.1 us
    all_to_all x1, blocking collectives, shards(): lax.all_to_all(parts.reshape(chips, CORES * own_rows, half + PAIR), 'seq'...  18.9 us
    pallas_call x1, Pallas kernels, shards(): pl.pallas_call(read_kernel, name='read', out_shape=jax.ShapeDtypeStruct((...  18.3 us
    all_to_all x1, waiting for transfers between devices, shards(): mixed = lax.all_to_all(mixed, 'seq', 0, 0, tiled=True)  8.87 us
    all_to_all x1, starting transfers between devices, shards(): first = lax.all_to_all(first, 'seq', 0, 0, tiled=True)  8.78 us
    all_to_all x1, starting transfers between devices, shards(): mixed = lax.all_to_all(mixed, 'seq', 0, 0, tiled=True)  6.95 us
    pallas_call x1, Pallas kernels, shards(): pl.pallas_call(query_kernel, name='query', grid=(1,), out_shape=jax.Shape...  5.33 us
  transfers between devices with their start and end apart: 4, of which 2 were waited for; matrix products, arithmetic and copies ran while one was open for 3% of the time, Pallas kernels for 17%

profile of v3, /device:TPU:1, one launch (start us, length us, event | category | flops | bytes accessed | tf_op | source)
XLA Modules:
  0.0 155.6 jit_solution(13638495537389579199)
XLA Ops:
  7.2 0.0 all-gather.2.cloned.1.call-start
  7.2 2.6 %pack.1 = (bf16[16,2,24,1664]{3,2,1,0:T(8,128)(2,1)}, bf16[9,24,768]{2,1,0:T(8,128)(2,1)}) custom-call(bf16[4,24,768]{2,1,0:T(8,128)(2,1)} %read_ref.1, bf16[8,24,768]{2,1,0:T(8,128)(2,1)} %later_ref.1, bf16[16,768]{1,0:T(8,128)(2,1)} %lat_ref.1), custom_call_target="tpu_custom_call" | custom-call | tf_op jit(solution)/shard_map/pack/pallas_call | solution.py:317
  9.8 0.0 all-gather.2.cloned.1.call-update
  9.9 0.0 copy-start
  9.9 8.8 %all-to-all-start = ((bf16[32,24,1664]{2,1,0:T(8,128)(2,1)}), bf16[32,24,1664]{2,1,0:T(8,128)(2,1)}, u32[]{:S(2)}, u32[]{:S(2)}) async-start(bf16[32,24,1664]{2,1,0:T(8,128)(2,1)} %bitcast.11), calls=%async_computation | async-start | bytes 5111808 | tf_op jit(solution)/shard_map/all_to_all | solution.py:329
  18.7 0.0 copy-done
  18.7 0.4 fusion
  19.1 0.3 fusion.1.own_ref.tok_ref
  19.4 0.0 copy-start.3
  19.4 0.4 collective-permute-start
  19.8 36.5 %all-to-all-done = bf16[32,24,1664]{2,1,0:T(8,128)(2,1)} async-done(((bf16[32,24,1664]{2,1,0:T(8,128)(2,1)}), bf16[32,24,1664]{2,1,0:T(8,128)(2,1)}, u32[]{:S(2)}, u32[]{:S(2)}) %all-to-all-start) | async-done | bytes 2555936 | tf_op jit(solution)/shard_map/all_to_all | solution.py:329
  56.3 1.1 slice.18
  57.4 1.0 fusion.2
  58.4 0.2 multiply_reduce_fusion
  58.6 0.0 copy-done.3
  58.6 0.0 copy-start.1
  58.7 0.1 rsqrt.21
  58.7 1.1 multiply_convert_fusion.lat_ref
  59.8 0.0 collective-permute-done.peer_ref
  59.8 18.3 %read.1 = bf16[512,512]{1,0:T(8,128)(2,1)} custom-call(s32[1]{0:T(128)} %bitcast.1.core_ref, f32[3,12]{1,0:T(4,128)} %scale_ref.3, bf16[1024,768]{1,0:T(8,128)(2,1)} %copy-done.3, bf16[1024,768]{1,0:T(8,128)(2,1)} %collective-permute-done.peer_ref, bf16[512,768]{1,0:T(8,128)(2,1)} %multiply_convert_fusion.lat_ref, bf16[768,1664]{1,0:T(8,128)(2,1)} %bitcast.4.weight_ref), custom_call_target="tpu_custom_call" | custom-call | flops 20000000000 | bytes 8000000 | tf_op jit(solution)/shard_map/read/pallas_call | solution.py:336
  78.2 0.0 copy-done.1
  78.2 18.9 %all_to_all.15 = bf16[16,32,512]{2,1,0:T(8,128)(2,1)} all-to-all(bf16[16,32,512]{2,1,0:T(8,128)(2,1)} %bitcast.13), channel_id=1, replica_groups={{0,16,32,48,64,80,96,112,128,144,160,176,192,208,224,240},{8,24,40,56,7..., dimensions={0} | all-to-all | bytes 1048576 | tf_op jit(solution)/shard_map/all_to_all | solution.py:368
  97.1 2.5 %combine.1 = bf16[32,32,384]{2,1,0:T(8,128)(2,1)} custom-call(bf16[512,512]{1,0:T(8,128)(2,1)} %bitcast.12), custom_call_target="tpu_custom_call" | custom-call | tf_op jit(solution)/shard_map/combine/pallas_call | solution.py:376
  99.5 7.0 %all-to-all-start.2 = ((bf16[32,32,384]{2,1,0:T(8,128)(2,1)}), bf16[32,32,384]{2,1,0:T(8,128)(2,1)S(1)}, u32[]{:S(2)}, u32[]{:S(2)}) async-start(bf16[32,32,384]{2,1,0:T(8,128)(2,1)} %combine.1), calls=%async_computation.2 | async-start | bytes 1572864 | tf_op jit(solution)/shard_map/all_to_all | solution.py:384
  106.5 0.0 all-gather.2.cloned.1.call-done.weight_ref.weights_ref
  106.5 5.3 %query.1.query_hbm_ref = bf16[1024,768]{1,0:T(8,128)(2,1)} custom-call(bf16[1024,768]{1,0:T(8,128)(2,1)} %copy-done.3, bf16[9,768,768]{2,1,0:T(8,128)(2,1)} %all-gather.2.cloned.1.call-done.weight_ref.weights_ref), custom_call_target="tpu_custom_call" | custom-call | flops 4000000000 | bytes 5000000 | tf_op jit(solution)/shard_map/query/pallas_call | solution.py:353
  111.8 8.9 %all-to-all-done.2 = bf16[32,32,384]{2,1,0:T(8,128)(2,1)S(1)} async-done(((bf16[32,32,384]{2,1,0:T(8,128)(2,1)}), bf16[32,32,384]{2,1,0:T(8,128)(2,1)S(1)}, u32[]{:S(2)}, u32[]{:S(2)}) %all-to-all-start.2) | async-done | bytes 786464 | tf_op jit(solution)/shard_map/all_to_all | solution.py:384
  120.7 0.0 copy-start.2
  120.7 0.9 copy-done.2
  121.6 27.1 %write.1 = (bf16[1024,768]{1,0:T(8,128)(2,1)}, f32[16,768]{1,0:T(8,128)}) custom-call(s32[1]{0:T(128)} %bitcast.index_ref, f32[3,12]{1,0:T(4,128)} %scale_ref.3, bf16[16,2,32,384]{3,2,1,0:T(8,128)(2,1)} %bitcast.10, bf16[512,768]{1,0:T(8,128)(2,1)} %bitcast.9, bf16[9,768,768]{2,1,0:T(8,128)(2,1)} %all-gather.2.cloned.1.call-done.weight_ref.weights_ref, ...), custom_call_target="tpu_custom_call" | custom-call | tf_op jit(solution)/shard_map/write/pallas_call | solution.py:388
  (2 shorter events, 0.0 us)
Async XLA Ops:
  7.2 99.3 %all-gather.2.cloned.1.call-start = ((), (), s32[]{:S(2)}) async-start(), calls=%async_computation.3 | async-start | bytes 10948608 | tf_op jit(solution)/shard_map/all_gather | solution.py:332
  9.9 8.8 %copy-start = (bf16[1024,768]{1,0:T(8,128)(2,1)S(1)}, bf16[1024,768]{1,0:T(8,128)(2,1)}, u32[]{:S(2)}) copy-start(bf16[1024,768]{1,0:T(8,128)(2,1)} %raw_hbm_ref.1) | copy-start | bytes 4718596
  9.9 46.4 %all-to-all-start = ((bf16[32,24,1664]{2,1,0:T(8,128)(2,1)}), bf16[32,24,1664]{2,1,0:T(8,128)(2,1)}, u32[]{:S(2)}, u32[]{:S(2)}) async-start(bf16[32,24,1664]{2,1,0:T(8,128)(2,1)} %bitcast.11), calls=%async_computation | async-start | bytes 5111808 | tf_op jit(solution)/shard_map/all_to_all | solution.py:329
  19.4 39.2 %copy-start.3 = (bf16[1024,768]{1,0:T(8,128)(2,1)}, bf16[1024,768]{1,0:T(8,128)(2,1)S(1)}, u32[]{:S(2)}) copy-start(bf16[1024,768]{1,0:T(8,128)(2,1)S(1)} %fusion.1.own_ref.tok_ref) | copy-start | bytes 4718596
  19.4 40.4 %collective-permute-start = (bf16[1024,768]{1,0:T(8,128)(2,1)S(1)}, bf16[1024,768]{1,0:T(8,128)(2,1)}, u32[]{:S(2)}, u32[]{:S(2)}) collective-permute-start(bf16[1024,768]{1,0:T(8,128)(2,1)S(1)} %fusion.1.own_ref.tok_ref), channel_id=1, source_target_pairs={{0,8},{8,0},{16,24},{24,16},{32,40},{40,32},{48,56},{56,48},{64,72... | collective-permute-start | bytes 4718600 | tf_op jit(solution)/shard_map/ppermute | solution.py:334
  58.6 19.6 %copy-start.1 = (bf16[32,16,768]{2,1,0:T(8,128)(2,1)}, bf16[32,16,768]{2,1,0:T(8,128)(2,1)S(1)}, u32[]{:S(2)}) copy-start(bf16[32,16,768]{2,1,0:T(8,128)(2,1)S(1)} %get-tuple-element.7) | copy-start | bytes 2359300
  99.5 21.2 %all-to-all-start.2 = ((bf16[32,32,384]{2,1,0:T(8,128)(2,1)}), bf16[32,32,384]{2,1,0:T(8,128)(2,1)S(1)}, u32[]{:S(2)}, u32[]{:S(2)}) async-start(bf16[32,32,384]{2,1,0:T(8,128)(2,1)} %combine.1), calls=%async_computation.2 | async-start | bytes 1572864 | tf_op jit(solution)/shard_map/all_to_all | solution.py:384
  120.7 0.9 copy-start.2
Sparse Core Ops, SparseCore 0:
  10.7 88.3 all-gather.1
